TPU v7x, 256 devices: a whole 4x4x8 slice. The times are simulated.
256 devices in a mesh: gx: 8 (over x, z_lo), gy: 32 (over y, z_hi, core).
Axes of the slice: x: 4, y: 4, z: 8 (z_hi: 4, z_lo: 2; z = z_hi * 2 + z_lo), core: 2. Of those that a mesh axis runs over, the one named last changes fastest.
Arguments:
- embeddings: bfloat16 [262144, 1024], P(('gx', 'gy')), may hold values from -7 to 7
Outputs:
- log_density: float32 [262144], P(('gx', 'gy'))
All inputs are finite; a program needn't handle non-finite values.
Results may differ from a plain program's by a relative error of at most 0.0003.
Values may be sent and summed in bfloat16 or wider, within the bound.
No kernel may reach another device: no remote copies, remote signals or barrier semaphores. Data moves between devices by JAX's collectives and lax.ppermute only.
A program may use at most 64 MiB of HBM per device.

v0:
```python
import functools
import math

import jax
import jax.numpy as jnp
from jax import lax
from jax.experimental import pallas as pl
from jax.experimental.pallas import tpu as pltpu
from jax.sharding import PartitionSpec as P

BAND = 64
LOG2E = math.log2(math.e)
HALF = 512
TILE = 256
LANES = 128
AXES = ("gx", "gy")
NX, NY, NZ = 4, 4, 8

DEVICES = [
    (x, y, z, c) for x in range(NX) for y in range(NY) for z in range(NZ) for c in range(2)
]


def number(x, y, z, c):
    x, y, z = x % NX, y % NY, z % NZ
    return (2 * x + z % 2) * 32 + 8 * y + 2 * (z // 2) + c


def is_first(x, y, z, c):
    return c != z % 2


def hop_one(x, y, z, c):
    return (x, y, z + 1, c) if c else (x, y, z - 1, c)


def hop_two(x, y, z, c):
    if c:
        t = (z + 1) % NZ
        return (x, y - (t in (3, 5)), t, c)
    t = (z - 1) % NZ
    return (x, y + (t in (2, 4)), t, c)


def hop_three(x, y, z, c):
    return (x, y, z - 1, c) if c else (x, y, z + 1, c)


def is_seam(x, y, z, c):
    return (z, c) in ((1, 1), (6, 0))


def own_across(x, y, z, c):
    if not is_first(x, y, z, c):
        return (x, y, z, 1 - c)
    return (x, y + (z in (2, 4, 6)), z, 0) if c else (x, y - (z in (1, 3, 5)), z, 1)


def own_in_plane(x, y, z, c):
    if is_first(x, y, z, c):
        return (x - 1, y - (z == 0), z, c) if c else (x + 1, y + (z == 7), z, c)
    if is_seam(x, y, z, c):
        return (x, y - 1, z, c) if c else (x, y + 1, z, c)
    return None


def two_along_x(x, y, z, c):
    if is_first(x, y, z, c):
        return None
    return (x + 1, y + 1, z, c) if c else (x - 1, y - 1, z, c)


def two_across(x, y, z, c):
    if not is_first(x, y, z, c):
        return None
    return (x, y + 1, z, 0) if c else (x, y - 1, z, 1)


def three_across(x, y, z, c):
    if is_first(x, y, z, c):
        return None
    return (x, y, z, 1 - c)


def route(*hops):
    pairs = []
    for source in DEVICES:
        at = source
        for hop in hops:
            at = at and hop(*at)
            at = at and (at[0] % NX, at[1] % NY, at[2] % NZ, at[3])
        if at:
            pairs.append((number(*source), number(*at)))
    return pairs


def back(pairs):
    return [(target, source) for source, target in pairs]


def move(value, pairs):
    return lax.ppermute(value, AXES, pairs)


def half_norms(block):
    values = block.astype(jnp.float32)
    return jnp.sum(values * values, axis=1) / (2.0 * BAND)


def kernel_block(left, left_half, right, right_half):
    inner = lax.dot_general(
        left, right, (((1,), (1,)), ((), ())), preferred_element_type=jnp.float32
    )
    return jnp.exp(inner / BAND - left_half[:, None] - right_half[None, :])


def lane_sums(values):
    return functools.reduce(
        lambda x, y: x + y,
        [values[:, i : i + LANES] for i in range(0, values.shape[1], LANES)],
    )


def as_row(partial):
    return jnp.sum(jnp.transpose(partial), axis=0, keepdims=True)


def pairs_kernel(parts_of, lefts_of, names, places, outs, has_single, flag, jobs, *refs):
    sources = dict(zip(names, refs[: len(names)]))
    results = dict(zip(outs, refs[len(names) : len(names) + len(outs)]))
    blocks, norms, rights, totals, sums, sems = refs[len(names) + len(outs) :]
    variant = flag[0]
    lefts = jnp.where(variant == 1, lefts_of[1], lefts_of[0])
    halves = jnp.where(variant == 1, len(parts_of[1]), len(parts_of[0]))

    for which in (0, 1):

        @pl.when(variant == which)
        def _(which=which):
            for slot, part in enumerate(parts_of[which]):
                name, offset = places[part]
                pltpu.make_async_copy(
                    sources[name].at[pl.ds(offset, HALF)], blocks.at[slot], sems.at[slot]
                ).start()

    def squares(slot):
        pltpu.make_async_copy(blocks.at[slot], blocks.at[slot], sems.at[slot]).wait()
        values = blocks[slot].astype(jnp.float32)
        return lane_sums(values * values) * (LOG2E / (2.0 * BAND))

    def prepare_left(slot, carry):
        norms[slot] = jnp.broadcast_to(
            jnp.sum(squares(slot), axis=1, keepdims=True), (HALF, LANES)
        )
        totals[slot] = jnp.zeros((HALF, LANES), jnp.float32)
        return carry

    def prepare_right(slot, carry):
        rights[slot] = as_row(squares(slot))
        sums[slot] = jnp.zeros((1, HALF), jnp.float32)
        return carry

    lax.fori_loop(0, lefts, prepare_left, 0)
    lax.fori_loop(lefts, halves, prepare_right, 0)

    def pair(left, right_slots):
        for right in right_slots:
            for at in range(0, HALF, TILE):
                inner = lax.dot_general(
                    blocks[left],
                    blocks[right, at : at + TILE],
                    (((1,), (1,)), ((), ())),
                    preferred_element_type=jnp.float32,
                )
                rows = None
                for lane in range(0, TILE, LANES):
                    cut = slice(at + lane, at + lane + LANES)
                    value = jnp.exp2(
                        inner[:, lane : lane + LANES] * (LOG2E / BAND)
                        - norms[left]
                        - rights[right, :, cut]
                    )
                    rows = value if rows is None else rows + value
                    sums[right, :, cut] += jnp.sum(value, axis=0, keepdims=True)
                totals[left] += rows

    def double(job, carry):
        pair(jobs[variant, 3 * job], (jobs[variant, 3 * job + 1], jobs[variant, 3 * job + 2]))
        return carry

    lax.fori_loop(0, jobs[variant, jobs.shape[1] - 1], double, 0)
    if has_single:
        single = jobs.shape[1] - 3

        @pl.when(jobs[variant, single] >= 0)
        def _():
            pair(jobs[variant, single], (jobs[variant, single + 1],))

    def finish(slot, carry):
        sums[slot] = as_row(totals[slot])
        return carry

    lax.fori_loop(0, lefts, finish, 0)

    for which in (0, 1):

        @pl.when(variant == which)
        def _(which=which):
            for part in outs:
                if part in parts_of[which]:
                    results[part][...] = sums[parts_of[which].index(part)]
                else:
                    results[part][...] = jnp.zeros_like(results[part])


def pair_sums(flag, arrays, jobs_first, jobs_second):
    names = list(arrays)
    places = {}
    for name in names:
        if arrays[name].shape[0] == HALF:
            places[name] = (name, 0)
        else:
            places[name + "0"], places[name + "1"] = (name, 0), (name, HALF)
    parts_of, lefts_of, rows = [], [], []
    lists = (jobs_second, jobs_first)
    most = max(len(jobs) for jobs in lists)
    for jobs in lists:
        left_parts = list(dict.fromkeys(job[0] for job in jobs))
        right_parts = list(dict.fromkeys(part for job in jobs for part in job[1:]))
        order = left_parts + right_parts
        parts_of.append(order)
        lefts_of.append(len(left_parts))
        doubles = [job for job in jobs if len(job) == 3]
        singles = [job for job in jobs if len(job) == 2]
        row = [order.index(part) for job in doubles for part in job]
        row += [0] * (3 * most - len(row))
        row += [order.index(part) for part in singles[0]] if singles else [-1, 0]
        rows.append(row + [len(doubles)])
    outs = sorted(set(parts_of[0]) | set(parts_of[1]))
    slots = max(len(order) for order in parts_of)
    has_single = any(len(job) == 2 for jobs in lists for job in jobs)
    smem = pl.BlockSpec(memory_space=pltpu.SMEM)
    results = pl.pallas_call(
        functools.partial(
            pairs_kernel, parts_of, lefts_of, names, places, outs, has_single
        ),
        out_shape=[jax.ShapeDtypeStruct((1, HALF), jnp.float32) for _ in outs],
        in_specs=[smem, smem] + [pl.BlockSpec(memory_space=pltpu.HBM)] * len(names),
        out_specs=[pl.BlockSpec(memory_space=pltpu.VMEM)] * len(outs),
        scratch_shapes=[
            pltpu.VMEM((slots, HALF, 1024), jnp.bfloat16),
            pltpu.VMEM((slots, HALF, LANES), jnp.float32),
            pltpu.VMEM((slots, 1, HALF), jnp.float32),
            pltpu.VMEM((slots, HALF, LANES), jnp.float32),
            pltpu.VMEM((slots, 1, HALF), jnp.float32),
            pltpu.SemaphoreType.DMA((slots,)),
        ],
        compiler_params=pltpu.CompilerParams(vmem_limit_bytes=32 * 1024 * 1024),
        cost_estimate=pl.CostEstimate(flops=1, bytes_accessed=1, transcendentals=0),
    )(flag, jnp.asarray(rows, jnp.int32), *[arrays[name] for name in names])
    return dict(zip(outs, results))


def both(lefts, first_right, second_right):
    return [(left, first_right, second_right) for left in lefts]


def whole(first_half, second_half):
    return jnp.concatenate([first_half[0], second_half[0]])


def after(value, *others):
    return lax.optimization_barrier((value, *others))[0]


def body(own):
    rows = own.shape[0]
    half = rows // 2
    first = lax.axis_index("gx") % 2 != lax.axis_index("gy") % 2

    gx, gy = lax.axis_index("gx"), lax.axis_index("gy")
    height, core = 2 * ((gy % 8) // 2) + gx % 2, gy % 2
    seam = ((height == 1) & (core == 1)) | ((height == 6) & (core == 0))
    flag = first.astype(jnp.int32).reshape(1)
    own_a = own[:half]
    own_b = lax.optimization_barrier(after(own, own_a)[half:])
    later = after(own, own_b)
    one_a = move(own_a, route(hop_one))
    one_b = move(own_b, route(hop_one))
    along = move(later, route(own_in_plane))
    across = move(later, route(own_across))
    two_a = move(one_a, route(hop_two))

    own_half = half_norms(own)
    diagonal = lax.broadcasted_iota(jnp.int32, (rows, rows), 0) == lax.broadcasted_iota(
        jnp.int32, (rows, rows), 1
    )
    same = jnp.where(diagonal, jnp.float32(0.0), kernel_block(own, own_half, own, own_half))
    total = jnp.sum(same, axis=1)
    two_b = move(after(one_b, total, own_half), route(hop_two))
    third_a, third_b = lax.optimization_barrier(
        (
            jnp.where(seam, along[:half], own[:half]),
            jnp.where(seam, along[half:], own[half:]),
        )
    )
    early = pair_sums(
        flag,
        dict(along=along, one_a=one_a, one_b=one_b),
        both(["along0", "along1"], "one_a", "one_b"),
        [],
    )

    two_a_after = after(two_a, early)
    two_c_a = move(two_a_after, route(two_across))
    two_x_a = move(two_a_after, route(two_along_x))
    three_a = move(after(third_a, two_a), route(hop_three))
    three_b = move(after(third_b, two_b), route(hop_three))
    two_c_b = move(two_b, route(two_across))
    two_x_b = move(after(two_b, two_x_a), route(two_along_x))

    middle = pair_sums(
        flag,
        dict(own=own, across=after(across, three_a), two_a=two_a, two_b=two_b, two_c_a=two_c_a),
        both(["own0", "own1"], "across0", "across1"),
        both(["across0", "across1", "two_c_a"], "two_a", "two_b"),
    )
    three_c_a = move(three_a, route(three_across))
    late = pair_sums(
        flag,
        dict(
            three_a=three_a, two_a=two_a, two_b=two_b, two_c_b=two_c_b, two_x_a=two_x_a,
            three_c_a=three_c_a,
        ),
        both(["three_a"], "two_a", "two_b") + [("three_a", "three_c_a")],
        both(["three_a", "two_c_b"], "two_a", "two_b") + [("three_a", "two_x_a")],
    )

    held = dict(route(own_in_plane))
    ahead = dict(route(hop_three))
    third = [(s, ahead[held[s] if is_seam(*PLACE[s]) else s]) for s in PLACE]
    over = dict(route(three_across))
    crossed = [(s, over[t]) for s, t in third if t in over]
    along_pairs = [p for p in route(own_in_plane) if is_first(*PLACE[p[1]])]
    one_pairs = [p for p in route(hop_one) if is_first(*PLACE[p[1]])]
    along_sums = move(whole(early["along0"], early["along1"]), back(along_pairs))
    across_sums = move(
        whole(middle["across0"], middle["across1"]), back(route(own_across))
    )

    three_b, _ = lax.optimization_barrier((three_b, (late, along_sums, across_sums)))
    three_c_b = move(three_b, route(three_across))
    last = pair_sums(
        flag,
        dict(
            three_b=three_b, two_a=two_a, two_b=two_b, two_x_a=two_x_a, two_x_b=two_x_b,
            three_a=three_a, three_c_a=three_c_a,
        ),
        both(["three_b"], "two_a", "two_b") + [("three_b", "three_c_a")],
        both(["three_b"], "two_a", "two_b")
        + both(["three_b"], "two_x_a", "two_x_b")
        + [("three_a", "two_x_b")],
    )
    final = pair_sums(
        flag,
        dict(three_a=three_a, three_b=three_b, three_c_b=three_c_b),
        both(["three_c_b"], "three_a", "three_b"),
        [],
    )

    total = total + whole(middle["own0"], middle["own1"])
    total = total + along_sums + across_sums
    total = total + move(
        after(
            whole(early["one_a"] + middle["two_c_a"], early["one_b"] + late["two_c_b"]), last
        ),
        back(one_pairs + route(hop_one, hop_two, two_across)),
    )
    total = total + move(
        whole(
            middle["two_a"] + late["two_a"] + last["two_a"],
            middle["two_b"] + late["two_b"] + last["two_b"],
        ),
        back(route(hop_one, hop_two)),
    )
    total = total + move(
        whole(
            late["three_a"] + last["three_a"] + final["three_a"],
            last["three_b"] + final["three_b"],
        ),
        back(third),
    )
    total = total + move(
        whole(
            late["two_x_a"] + last["two_x_a"] + late["three_c_a"] + last["three_c_a"],
            last["two_x_b"] + final["three_c_b"],
        ),
        back(crossed + route(hop_one, hop_two, two_along_x)),
    )
    return own_half + jnp.log(total)


PLACE = {number(*device): device for device in DEVICES}


def solution(mesh):
    in_specs = (P(AXES, None),)
    return jax.shard_map(
        body, mesh=mesh, in_specs=in_specs, out_specs=P(AXES), check_vma=False
    )
```

profile of v0, /device:TPU:128, one launch (start us, length us, event | category | flops | bytes accessed | tf_op | source)
XLA Modules:
  0.0 122.2 jit_solution(12880270072795476531)
XLA Ops:
  0.0 1.4 %slice.16 = bf16[512,1024]{1,0:T(8,128)(2,1)S(1)} slice(bf16[1024,1024]{1,0:T(8,128)(2,1)} %refs_0_.1), slice={[0:512], [0:1024]} | slice | bytes 2097152 | tf_op jit(solution)/shard_map/slice | solution.py:285
  1.4 0.5 copy-done
  1.9 1.0 slice.17
  3.0 2.0 %collective-permute-start.1 = (bf16[1024,1024]{1,0:T(8,128)(2,1)S(1)}, bf16[1024,1024]{1,0:T(8,128)(2,1)}, u32[]{:S(2)}, u32[]{:S(2)}) collective-permute-start(bf16[1024,1024]{1,0:T(8,128)(2,1)S(1)} %copy-done), channel_id=1, source_target_pairs={{1,217},{32,96},{33,57},{3,195},{34,98},{5,197},{36,100},{6,14},{7... | collective-permute-start | bytes 6291464 | tf_op jit(solution)/shard_map/ppermute | solution.py:102
  5.0 1.6 %collective-permute-start.2 = (bf16[512,1024]{1,0:T(8,128)(2,1)S(1)}, bf16[512,1024]{1,0:T(8,128)(2,1)}, u32[]{:S(2)}, u32[]{:S(2)}) collective-permute-start(bf16[512,1024]{1,0:T(8,128)(2,1)S(1)} %slice.16), channel_id=1, source_target_pairs={{0,38},{1,33},{32,0},{33,3},{2,32},{3,35},{34,2},{35,5},{4,34},{5,... | collective-permute-start | bytes 3145736 | tf_op jit(solution)/shard_map/ppermute | solution.py:102
  6.5 0.1 collective-permute-start.5
  6.6 2.1 %collective-permute-start = (bf16[1024,1024]{1,0:T(8,128)(2,1)S(1)}, bf16[1024,1024]{1,0:T(8,128)(2,1)}, u32[]{:S(2)}, u32[]{:S(2)}) collective-permute-start(bf16[1024,1024]{1,0:T(8,128)(2,1)S(1)} %copy-done), channel_id=1, source_target_pairs={{0,1},{1,0},{32,57},{33,32},{2,3},{3,10},{34,59},{35,34},{4,5},{5,... | collective-permute-start | bytes 6291464 | tf_op jit(solution)/shard_map/ppermute | solution.py:102
  8.7 0.5 multiply_reduce_fusion
  9.2 11.1 %collective-permute-done.2.refs_1_ = bf16[512,1024]{1,0:T(8,128)(2,1)} collective-permute-done((bf16[512,1024]{1,0:T(8,128)(2,1)S(1)}, bf16[512,1024]{1,0:T(8,128)(2,1)}, u32[]{:S(2)}, u32[]{:S(2)}) %collective-permute-start.2) | collective-permute-done | bytes 1048608 | tf_op jit(solution)/shard_map/ppermute | solution.py:102
  20.3 2.3 %collective-permute-start.3 = (bf16[512,1024]{1,0:T(8,128)(2,1)}, bf16[512,1024]{1,0:T(8,128)(2,1)S(1)}, u32[]{:S(2)}, u32[]{:S(2)}) collective-permute-start(bf16[512,1024]{1,0:T(8,128)(2,1)} %collective-permute-done.2.refs_1_), channel_id=1, source_target_pairs={{0,38},{1,33},{32,0},{33,3},{2,32},{3,59},{34,10},{35,5},{4,34},{5... | collective-permute-start | bytes 3145736 | tf_op jit(solution)/shard_map/ppermute | solution.py:102
  22.7 2.7 %select_reduce_fusion = f32[1024]{0:T(1024)S(1)} fusion(bf16[1024,1024]{1,0:T(8,128)(2,1)S(1)} %copy-done, f32[1024]{0:T(1024)S(1)} %broadcast_multiply_fusion), kind=kOutput, calls=%fused_computation | convolution fusion | flops 2153774080 | bytes 2105344 | tf_op jit(solution)/shard_map/dot_general | solution.py:111
  25.4 0.0 copy-start.4
  25.4 6.1 %collective-permute-done.5.refs_2_ = bf16[512,1024]{1,0:T(8,128)(2,1)} collective-permute-done((bf16[512,1024]{1,0:T(8,128)(2,1)}, bf16[512,1024]{1,0:T(8,128)(2,1)}, u32[]{:S(2)}, u32[]{:S(2)}) %collective-permute-start.5) | collective-permute-done | bytes 1048608 | tf_op jit(solution)/shard_map/ppermute | solution.py:102
  31.6 2.3 %collective-permute-start.6 = (bf16[512,1024]{1,0:T(8,128)(2,1)}, bf16[512,1024]{1,0:T(8,128)(2,1)S(1)}, u32[]{:S(2)}, u32[]{:S(2)}) collective-permute-start(bf16[512,1024]{1,0:T(8,128)(2,1)} %collective-permute-done.5.refs_2_), channel_id=1, source_target_pairs={{0,38},{1,33},{32,0},{33,3},{2,32},{3,59},{34,10},{35,5},{4,34},{5... | collective-permute-start | bytes 3145736 | tf_op jit(solution)/shard_map/ppermute | solution.py:102
  33.9 0.0 collective-permute-done.1.refs_0_
  33.9 1.7 %slice_select_fusion = (bf16[512,1024]{1,0:T(8,128)(2,1)S(1)}, bf16[512,1024]{1,0:T(8,128)(2,1)S(1)}) fusion(bf16[1024,1024]{1,0:T(8,128)(2,1)} %collective-permute-done.1.refs_0_, bf16[1024,1024]{1,0:T(8,128)(2,1)S(1)} %copy-done, pred[]{:T(512)S(6)} %or.3), kind=kLoop, calls=%fused_computation.3 | loop fusion | flops 1048576 | bytes 6291457 | tf_op jit(solution)/shard_map/jit(_where)/select_n | solution.py:304
  35.6 9.6 %collective-permute-done.3.refs_2_.refs_1_ = bf16[512,1024]{1,0:T(8,128)(2,1)S(1)} collective-permute-done((bf16[512,1024]{1,0:T(8,128)(2,1)}, bf16[512,1024]{1,0:T(8,128)(2,1)S(1)}, u32[]{:S(2)}, u32[]{:S(2)}) %collective-permute-start.3) | collective-permute-done | bytes 1048608 | tf_op jit(solution)/shard_map/ppermute | solution.py:102
  45.3 0.6 shard_map.64
  45.9 5.6 %collective-permute-start.11 = (bf16[512,1024]{1,0:T(8,128)(2,1)S(1)}, bf16[512,1024]{1,0:T(8,128)(2,1)S(1)}, u32[]{:S(2)}, u32[]{:S(2)}) collective-permute-start(bf16[512,1024]{1,0:T(8,128)(2,1)S(1)} %collective-permute-done.3.refs_2_.refs_1_), channel_id=1, source_target_pairs={{0,216},{33,105},{2,218},{35,107},{4,220},{37,109},{6,222},{39,111... | collective-permute-start | bytes 3145736 | tf_op jit(solution)/shard_map/ppermute | solution.py:102
  51.5 1.3 %collective-permute-start.7 = (bf16[512,1024]{1,0:T(8,128)(2,1)S(1)}, bf16[512,1024]{1,0:T(8,128)(2,1)S(1)}, u32[]{:S(2)}, u32[]{:S(2)}) collective-permute-start(bf16[512,1024]{1,0:T(8,128)(2,1)S(1)} %collective-permute-done.3.refs_2_.refs_1_), channel_id=1, source_target_pairs={{1,8},{32,57},{3,10},{34,59},{5,12},{36,61},{7,14},{38,63},{9,16},... | collective-permute-start | bytes 3145736 | tf_op jit(solution)/shard_map/ppermute | solution.py:102
  52.8 10.3 %collective-permute-done.6.refs_3_.refs_2_ = bf16[512,1024]{1,0:T(8,128)(2,1)S(1)} collective-permute-done((bf16[512,1024]{1,0:T(8,128)(2,1)}, bf16[512,1024]{1,0:T(8,128)(2,1)S(1)}, u32[]{:S(2)}, u32[]{:S(2)}) %collective-permute-start.6) | collective-permute-done | bytes 1048608 | tf_op jit(solution)/shard_map/ppermute | solution.py:102
  63.0 1.3 %collective-permute-start.10 = (bf16[512,1024]{1,0:T(8,128)(2,1)S(1)}, bf16[512,1024]{1,0:T(8,128)(2,1)S(1)}, u32[]{:S(2)}, u32[]{:S(2)}) collective-permute-start(bf16[512,1024]{1,0:T(8,128)(2,1)S(1)} %collective-permute-done.6.refs_3_.refs_2_), channel_id=1, source_target_pairs={{1,8},{32,57},{3,10},{34,59},{5,12},{36,61},{7,14},{38,63},{9,16},... | collective-permute-start | bytes 3145736 | tf_op jit(solution)/shard_map/ppermute | solution.py:102
  64.3 2.9 %collective-permute-done.4.refs_0_.refs_5_ = bf16[512,1024]{1,0:T(8,128)(2,1)S(1)} collective-permute-done((bf16[512,1024]{1,0:T(8,128)(2,1)S(1)}, bf16[512,1024]{1,0:T(8,128)(2,1)S(1)}, u32[]{:S(2)}, u32[]{:S(2)}) %collective-permute-start.4) | collective-permute-done | bytes 1048608 | tf_op jit(solution)/shard_map/ppermute | solution.py:102
  67.2 1.3 %collective-permute-start.12 = (bf16[512,1024]{1,0:T(8,128)(2,1)S(1)}, bf16[512,1024]{1,0:T(8,128)(2,1)S(1)}, u32[]{:S(2)}, u32[]{:S(2)}) collective-permute-start(bf16[512,1024]{1,0:T(8,128)(2,1)S(1)} %collective-permute-done.4.refs_0_.refs_5_), channel_id=1, source_target_pairs={{0,1},{33,32},{2,3},{35,34},{4,5},{37,36},{6,7},{39,38},{8,9},{41,... | collective-permute-start | bytes 3145736 | tf_op jit(solution)/shard_map/ppermute | solution.py:102
  68.6 0.0 collective-permute-done.11.refs_4_.refs_3_
  68.6 1.4 %collective-permute-start.13 = (bf16[512,1024]{1,0:T(8,128)(2,1)S(1)}, bf16[512,1024]{1,0:T(8,128)(2,1)S(1)}, u32[]{:S(2)}, u32[]{:S(2)}) collective-permute-start(bf16[512,1024]{1,0:T(8,128)(2,1)S(1)} %get-tuple-element.62), channel_id=1, source_target_pairs={{0,32},{1,39},{32,2},{33,1},{2,34},{3,33},{34,4},{35,3},{4,36},{5,... | collective-permute-start | bytes 3145736 | tf_op jit(solution)/shard_map/ppermute | solution.py:102
  70.0 6.4 %collective-permute-start.14 = (bf16[512,1024]{1,0:T(8,128)(2,1)S(1)}, bf16[512,1024]{1,0:T(8,128)(2,1)S(1)}, u32[]{:S(2)}, u32[]{:S(2)}) collective-permute-start(bf16[512,1024]{1,0:T(8,128)(2,1)S(1)} %collective-permute-done.6.refs_3_.refs_2_), channel_id=1, source_target_pairs={{0,216},{33,105},{2,218},{35,107},{4,220},{37,109},{6,222},{39,111... | collective-permute-start | bytes 3145736 | tf_op jit(solution)/shard_map/ppermute | solution.py:102
  76.5 0.0 copy-start.5
  76.5 0.0 collective-permute-done.7.refs_4_
  76.5 0.7 collective-permute-start.8
  77.2 8.2 %shard_map.65 = (f32[1,512]{1,0:T(1,128)S(1)}, f32[1,512]{1,0:T(1,128)S(1)}, f32[1,512]{1,0:T(1,128)S(1)}, f32[1,512]{1,0:T(1,128)S(1)}, f32[1,512]{1,0:T(1,128)...) custom-call(s32[1]{0:T(128)} %bitcast.flag, s32[2,12]{1,0:T(2,128)S(1)} %copy-done.3, bf16[1024,1024]{1,0:T(8,128)(2,1)S(1)} %copy-done, ...), custom_call_target="tpu_custom_call" | custom-call | flops 1 | bytes 1 | tf_op jit(solution)/shard_map/pallas_call | solution.py:243
  85.4 0.0 copy-start.2
  85.4 0.0 collective-permute-done.10.refs_3_
  85.4 0.1 collective-permute-start.9
  85.5 0.0 collective-permute-done.12.refs_5_.refs_6_
  85.6 6.5 %shard_map.66 = (f32[1,512]{1,0:T(1,128)S(1)}, f32[1,512]{1,0:T(1,128)S(1)}, f32[1,512]{1,0:T(1,128)S(1)}, f32[1,512]{1,0:T(1,128)S(1)}, f32[1,512]{1,0:T(1,128)S(1)}, /*index=5*/f32[1,512]{1,0:T(1,128)S(1)}) custom-call(s32[1]{0:T(128)} %bitcast.flag, s32[2,12]{1,0:T(2,128)S(1)} %copy-done.5, bf16[512,1024]{1,0:T(8,128)(2,1)S(1)} %collective-permute-done.4.refs_0_.refs_5_, ...), custom_call_target="tpu_custom_call" | custom-call | flops 1 | bytes 1 | tf_op jit(solution)/shard_map/pallas_call | solution.py:243
  92.1 0.0 collective-permute-done.9
  92.1 1.4 %collective-permute-start.17 = (bf16[512,1024]{1,0:T(8,128)(2,1)S(1)}, bf16[512,1024]{1,0:T(8,128)(2,1)S(1)}, u32[]{:S(2)}, u32[]{:S(2)}) collective-permute-start(bf16[512,1024]{1,0:T(8,128)(2,1)S(1)} %collective-permute-done.13.refs_0_.refs_1_), channel_id=1, source_target_pairs={{0,1},{33,32},{2,3},{35,34},{4,5},{37,36},{6,7},{39,38},{8,9},{41,... | collective-permute-start | bytes 3145736 | tf_op jit(solution)/shard_map/ppermute | solution.py:102
  93.5 0.0 copy-start.1
  93.5 6.9 %shard_map.67 = (f32[1,512]{1,0:T(1,128)S(1)}, f32[1,512]{1,0:T(1,128)S(1)}, f32[1,512]{1,0:T(1,128)S(1)}, f32[1,512]{1,0:T(1,128)S(1)}, f32[1,512]{1,0:T(1,128)...) custom-call(s32[1]{0:T(128)} %bitcast.flag, s32[2,12]{1,0:T(2,128)S(1)} %copy-done.2, ...), custom_call_target="tpu_custom_call" | custom-call | flops 1 | bytes 1 | tf_op jit(solution)/shard_map/pallas_call | solution.py:243
  100.4 0.1 collective-permute-start.15
  100.5 5.5 %collective-permute-start.16 = (f32[1024]{0:T(1024)S(1)}, f32[1024]{0:T(1024)S(1)}, u32[]{:S(2)}, u32[]{:S(2)}) collective-permute-start(f32[1024]{0:T(1024)S(1)} %pad_maximum_fusion.3), channel_id=1, source_target_pairs={{6,0},{3,1},{38,32},{59,33},{0,2},{5,3},{32,34},{61,35},{10,4},{7,... | collective-permute-start | bytes 12296 | tf_op jit(solution)/shard_map/ppermute | solution.py:102
  106.0 0.6 shard_map.68
  106.7 7.0 %collective-permute-start.18 = (f32[1024]{0:T(1024)S(1)}, f32[1024]{0:T(1024)S(1)}, u32[]{:S(2)}, u32[]{:S(2)}) collective-permute-start(f32[1024]{0:T(1024)S(1)} %pad_maximum_fusion.4), channel_id=1, source_target_pairs={{32,0},{39,1},{2,32},{25,33},{34,2},{33,3},{4,34},{3,35},{36,4},{3... | collective-permute-start | bytes 12296 | tf_op jit(solution)/shard_map/ppermute | solution.py:102
  113.7 0.1 collective-permute-start.19
  113.8 1.2 collective-permute-done.18
  115.0 6.6 %collective-permute-done.19 = f32[1024]{0:T(1024)S(1)} collective-permute-done((f32[1024]{0:T(1024)S(1)}, f32[1024]{0:T(1024)S(1)}, u32[]{:S(2)}, u32[]{:S(2)}) %collective-permute-start.19) | collective-permute-done | bytes 4128 | tf_op jit(solution)/shard_map/ppermute | solution.py:102
  121.6 0.6 fusion.7
  (28 shorter events, 0.1 us)
Async XLA Ops:
  0.0 1.9 %copy-start = (bf16[1024,1024]{1,0:T(8,128)(2,1)S(1)}, bf16[1024,1024]{1,0:T(8,128)(2,1)}, u32[]{:S(2)}) copy-start(bf16[1024,1024]{1,0:T(8,128)(2,1)} %refs_0_.1) | copy-start | bytes 6291460
  3.0 30.9 %collective-permute-start.1 = (bf16[1024,1024]{1,0:T(8,128)(2,1)S(1)}, bf16[1024,1024]{1,0:T(8,128)(2,1)}, u32[]{:S(2)}, u32[]{:S(2)}) collective-permute-start(bf16[1024,1024]{1,0:T(8,128)(2,1)S(1)} %copy-done), channel_id=1, source_target_pairs={{1,217},{32,96},{33,57},{3,195},{34,98},{5,197},{36,100},{6,14},{7... | collective-permute-start | bytes 6291464 | tf_op jit(solution)/shard_map/ppermute | solution.py:102
  5.0 15.4 %collective-permute-start.2 = (bf16[512,1024]{1,0:T(8,128)(2,1)S(1)}, bf16[512,1024]{1,0:T(8,128)(2,1)}, u32[]{:S(2)}, u32[]{:S(2)}) collective-permute-start(bf16[512,1024]{1,0:T(8,128)(2,1)S(1)} %slice.16), channel_id=1, source_target_pairs={{0,38},{1,33},{32,0},{33,3},{2,32},{3,35},{34,2},{35,5},{4,34},{5,... | collective-permute-start | bytes 3145736 | tf_op jit(solution)/shard_map/ppermute | solution.py:102
  6.5 25.0 %collective-permute-start.5 = (bf16[512,1024]{1,0:T(8,128)(2,1)}, bf16[512,1024]{1,0:T(8,128)(2,1)}, u32[]{:S(2)}, u32[]{:S(2)}) collective-permute-start(bf16[512,1024]{1,0:T(8,128)(2,1)} %slice.17), channel_id=1, source_target_pairs={{0,38},{1,33},{32,0},{33,3},{2,32},{3,35},{34,2},{35,5},{4,34},{5,... | collective-permute-start | bytes 3145736 | tf_op jit(solution)/shard_map/ppermute | solution.py:102
  6.6 63.4 %collective-permute-start = (bf16[1024,1024]{1,0:T(8,128)(2,1)S(1)}, bf16[1024,1024]{1,0:T(8,128)(2,1)}, u32[]{:S(2)}, u32[]{:S(2)}) collective-permute-start(bf16[1024,1024]{1,0:T(8,128)(2,1)S(1)} %copy-done), channel_id=1, source_target_pairs={{0,1},{1,0},{32,57},{33,32},{2,3},{3,10},{34,59},{35,34},{4,5},{5,... | collective-permute-start | bytes 6291464 | tf_op jit(solution)/shard_map/ppermute | solution.py:102
  20.3 24.9 %collective-permute-start.3 = (bf16[512,1024]{1,0:T(8,128)(2,1)}, bf16[512,1024]{1,0:T(8,128)(2,1)S(1)}, u32[]{:S(2)}, u32[]{:S(2)}) collective-permute-start(bf16[512,1024]{1,0:T(8,128)(2,1)} %collective-permute-done.2.refs_1_), channel_id=1, source_target_pairs={{0,38},{1,33},{32,0},{33,3},{2,32},{3,59},{34,10},{35,5},{4,34},{5... | collective-permute-start | bytes 3145736 | tf_op jit(solution)/shard_map/ppermute | solution.py:102
  25.4 19.8 %copy-start.4 = (s32[2,9]{1,0:T(2,128)S(1)}, s32[2,9]{1,0:T(2,128)}, u32[]{:S(2)}) copy-start(s32[2,9]{1,0:T(2,128)} %constant.73.clone.jobs) | copy-start | bytes 220
  31.6 31.5 %collective-permute-start.6 = (bf16[512,1024]{1,0:T(8,128)(2,1)}, bf16[512,1024]{1,0:T(8,128)(2,1)S(1)}, u32[]{:S(2)}, u32[]{:S(2)}) collective-permute-start(bf16[512,1024]{1,0:T(8,128)(2,1)} %collective-permute-done.5.refs_2_), channel_id=1, source_target_pairs={{0,38},{1,33},{32,0},{33,3},{2,32},{3,59},{34,10},{35,5},{4,34},{5... | collective-permute-start | bytes 3145736 | tf_op jit(solution)/shard_map/ppermute | solution.py:102
  45.2 22.0 %collective-permute-start.4 = (bf16[512,1024]{1,0:T(8,128)(2,1)S(1)}, bf16[512,1024]{1,0:T(8,128)(2,1)S(1)}, u32[]{:S(2)}, u32[]{:S(2)}) collective-permute-start(bf16[512,1024]{1,0:T(8,128)(2,1)S(1)} %get-tuple-element.47), channel_id=1, source_target_pairs={{0,32},{1,39},{32,2},{33,1},{2,34},{3,33},{34,4},{35,3},{4,36},{5,... | collective-permute-start | bytes 3145736 | tf_op jit(solution)/shard_map/ppermute | solution.py:102
  45.3 32.0 %copy-start.3 = (s32[2,12]{1,0:T(2,128)S(1)}, s32[2,12]{1,0:T(2,128)}, u32[]{:S(2)}) copy-start(s32[2,12]{1,0:T(2,128)} %constant.74.clone.jobs) | copy-start | bytes 292
  45.9 22.7 %collective-permute-start.11 = (bf16[512,1024]{1,0:T(8,128)(2,1)S(1)}, bf16[512,1024]{1,0:T(8,128)(2,1)S(1)}, u32[]{:S(2)}, u32[]{:S(2)}) collective-permute-start(bf16[512,1024]{1,0:T(8,128)(2,1)S(1)} %collective-permute-done.3.refs_2_.refs_1_), channel_id=1, source_target_pairs={{0,216},{33,105},{2,218},{35,107},{4,220},{37,109},{6,222},{39,111... | collective-permute-start | bytes 3145736 | tf_op jit(solution)/shard_map/ppermute | solution.py:102
  51.5 25.1 %collective-permute-start.7 = (bf16[512,1024]{1,0:T(8,128)(2,1)S(1)}, bf16[512,1024]{1,0:T(8,128)(2,1)S(1)}, u32[]{:S(2)}, u32[]{:S(2)}) collective-permute-start(bf16[512,1024]{1,0:T(8,128)(2,1)S(1)} %collective-permute-done.3.refs_2_.refs_1_), channel_id=1, source_target_pairs={{1,8},{32,57},{3,10},{34,59},{5,12},{36,61},{7,14},{38,63},{9,16},... | collective-permute-start | bytes 3145736 | tf_op jit(solution)/shard_map/ppermute | solution.py:102
  63.0 22.4 %collective-permute-start.10 = (bf16[512,1024]{1,0:T(8,128)(2,1)S(1)}, bf16[512,1024]{1,0:T(8,128)(2,1)S(1)}, u32[]{:S(2)}, u32[]{:S(2)}) collective-permute-start(bf16[512,1024]{1,0:T(8,128)(2,1)S(1)} %collective-permute-done.6.refs_3_.refs_2_), channel_id=1, source_target_pairs={{1,8},{32,57},{3,10},{34,59},{5,12},{36,61},{7,14},{38,63},{9,16},... | collective-permute-start | bytes 3145736 | tf_op jit(solution)/shard_map/ppermute | solution.py:102
  67.2 18.3 %collective-permute-start.12 = (bf16[512,1024]{1,0:T(8,128)(2,1)S(1)}, bf16[512,1024]{1,0:T(8,128)(2,1)S(1)}, u32[]{:S(2)}, u32[]{:S(2)}) collective-permute-start(bf16[512,1024]{1,0:T(8,128)(2,1)S(1)} %collective-permute-done.4.refs_0_.refs_5_), channel_id=1, source_target_pairs={{0,1},{33,32},{2,3},{35,34},{4,5},{37,36},{6,7},{39,38},{8,9},{41,... | collective-permute-start | bytes 3145736 | tf_op jit(solution)/shard_map/ppermute | solution.py:102
  68.6 23.5 %collective-permute-start.13 = (bf16[512,1024]{1,0:T(8,128)(2,1)S(1)}, bf16[512,1024]{1,0:T(8,128)(2,1)S(1)}, u32[]{:S(2)}, u32[]{:S(2)}) collective-permute-start(bf16[512,1024]{1,0:T(8,128)(2,1)S(1)} %get-tuple-element.62), channel_id=1, source_target_pairs={{0,32},{1,39},{32,2},{33,1},{2,34},{3,33},{34,4},{35,3},{4,36},{5,... | collective-permute-start | bytes 3145736 | tf_op jit(solution)/shard_map/ppermute | solution.py:102
  70.0 23.5 %collective-permute-start.14 = (bf16[512,1024]{1,0:T(8,128)(2,1)S(1)}, bf16[512,1024]{1,0:T(8,128)(2,1)S(1)}, u32[]{:S(2)}, u32[]{:S(2)}) collective-permute-start(bf16[512,1024]{1,0:T(8,128)(2,1)S(1)} %collective-permute-done.6.refs_3_.refs_2_), channel_id=1, source_target_pairs={{0,216},{33,105},{2,218},{35,107},{4,220},{37,109},{6,222},{39,111... | collective-permute-start | bytes 3145736 | tf_op jit(solution)/shard_map/ppermute | solution.py:102
  76.5 9.0 %copy-start.5 = (s32[2,12]{1,0:T(2,128)S(1)}, s32[2,12]{1,0:T(2,128)}, u32[]{:S(2)}) copy-start(s32[2,12]{1,0:T(2,128)} %constant.75.clone.jobs) | copy-start | bytes 292
  76.5 15.5 %collective-permute-start.8 = (f32[1024]{0:T(1024)S(1)}, f32[1024]{0:T(1024)S(1)}, u32[]{:S(2)}, u32[]{:S(2)}) collective-permute-start(f32[1024]{0:T(1024)S(1)} %pad_maximum_fusion), channel_id=1, source_target_pairs={{217,1},{96,32},{195,3},{98,34},{197,5},{100,36},{199,7},{110,38},... | collective-permute-start | bytes 12296 | tf_op jit(solution)/shard_map/ppermute | solution.py:102
  85.4 8.1 %copy-start.2 = (s32[2,12]{1,0:T(2,128)S(1)}, s32[2,12]{1,0:T(2,128)}, u32[]{:S(2)}) copy-start(s32[2,12]{1,0:T(2,128)} %constant.76.clone.jobs) | copy-start | bytes 292
  85.4 6.6 %collective-permute-start.9 = (f32[1024]{0:T(1024)S(1)}, f32[1024]{0:T(1024)S(1)}, u32[]{:S(2)}, u32[]{:S(2)}) collective-permute-start(f32[1024]{0:T(1024)S(1)} %pad_maximum_fusion.1), channel_id=1, source_target_pairs={{1,0},{0,1},{57,32},{32,33},{3,2},{10,3},{59,34},{34,35},{5,4},{12... | collective-permute-start | bytes 12296 | tf_op jit(solution)/shard_map/ppermute | solution.py:102
  92.1 13.9 %collective-permute-start.17 = (bf16[512,1024]{1,0:T(8,128)(2,1)S(1)}, bf16[512,1024]{1,0:T(8,128)(2,1)S(1)}, u32[]{:S(2)}, u32[]{:S(2)}) collective-permute-start(bf16[512,1024]{1,0:T(8,128)(2,1)S(1)} %collective-permute-done.13.refs_0_.refs_1_), channel_id=1, source_target_pairs={{0,1},{33,32},{2,3},{35,34},{4,5},{37,36},{6,7},{39,38},{8,9},{41,... | collective-permute-start | bytes 3145736 | tf_op jit(solution)/shard_map/ppermute | solution.py:102
  93.5 12.5 %copy-start.1 = (s32[2,6]{1,0:T(2,128)S(1)}, s32[2,6]{1,0:T(2,128)}, u32[]{:S(2)}) copy-start(s32[2,6]{1,0:T(2,128)} %constant.77.clone.jobs) | copy-start | bytes 148
  100.4 13.4 %collective-permute-start.15 = (f32[1024]{0:T(1024)S(1)}, f32[1024]{0:T(1024)S(1)}, u32[]{:S(2)}, u32[]{:S(2)}) collective-permute-start(f32[1024]{0:T(1024)S(1)} %pad_maximum_fusion.2), channel_id=1, source_target_pairs={{38,0},{3,33},{32,2},{5,35},{34,4},{7,37},{36,6},{1,39},{46,8},{11... | collective-permute-start | bytes 12296 | tf_op jit(solution)/shard_map/ppermute | solution.py:102
  100.5 13.3 %collective-permute-start.16 = (f32[1024]{0:T(1024)S(1)}, f32[1024]{0:T(1024)S(1)}, u32[]{:S(2)}, u32[]{:S(2)}) collective-permute-start(f32[1024]{0:T(1024)S(1)} %pad_maximum_fusion.3), channel_id=1, source_target_pairs={{6,0},{3,1},{38,32},{59,33},{0,2},{5,3},{32,34},{61,35},{10,4},{7,... | collective-permute-start | bytes 12296 | tf_op jit(solution)/shard_map/ppermute | solution.py:102
  106.7 8.3 %collective-permute-start.18 = (f32[1024]{0:T(1024)S(1)}, f32[1024]{0:T(1024)S(1)}, u32[]{:S(2)}, u32[]{:S(2)}) collective-permute-start(f32[1024]{0:T(1024)S(1)} %pad_maximum_fusion.4), channel_id=1, source_target_pairs={{32,0},{39,1},{2,32},{25,33},{34,2},{33,3},{4,34},{3,35},{36,4},{3... | collective-permute-start | bytes 12296 | tf_op jit(solution)/shard_map/ppermute | solution.py:102
  113.7 7.9 %collective-permute-start.19 = (f32[1024]{0:T(1024)S(1)}, f32[1024]{0:T(1024)S(1)}, u32[]{:S(2)}, u32[]{:S(2)}) collective-permute-start(f32[1024]{0:T(1024)S(1)} %pad_maximum_fusion.5), channel_id=1, source_target_pairs={{38,1},{3,32},{32,3},{5,34},{34,5},{7,36},{36,7},{1,38},{46,9},{11... | collective-permute-start | bytes 12296 | tf_op jit(solution)/shard_map/ppermute | solution.py:102
where the time goes:
time: 123 us; the launch traced here: 122 us
  waiting for transfers between devices  47.9 us (39%)
  starting transfers between devices  42.5 us (35%)
  Pallas kernels  22.8 us (19%)
  local copies, waits for them, and re-layouts  2.98 us (2%)
  other arithmetic  2.93 us (2%)
  matrix products  2.69 us (2%)
    ppermute x20, waiting for transfers between devices, move(): return lax.ppermute(value, AXES, pairs)  47.9 us
    ppermute x20, starting transfers between devices, move(): return lax.ppermute(value, AXES, pairs)  42.5 us
    pallas_call x5, Pallas kernels, pair_sums(): pl.pallas_call(functools.partial(pairs_kernel, parts_of, lefts_of, names,...  22.8 us
    dot_general x1, matrix products, kernel_block(): lax.dot_general(left, right, (((1,), (1,)), ((), ())), preferred_element_...  2.69 us
  transfers between devices with their start and end apart: 20, of which 7 were waited for; matrix products, arithmetic and copies ran while one was open for 4% of the time, Pallas kernels for 19%

commit v1 on v0

--- a/solution.py
+++ b/solution.py
@@ -125,95 +125,84 @@
     return jnp.sum(jnp.transpose(partial), axis=0, keepdims=True)
 
 
-def pairs_kernel(parts_of, lefts_of, names, places, outs, has_single, flag, jobs, *refs):
+def pairs_kernel(parts_of, jobs, names, places, outs, flag, *refs):
     sources = dict(zip(names, refs[: len(names)]))
     results = dict(zip(outs, refs[len(names) : len(names) + len(outs)]))
     blocks, norms, rights, totals, sums, sems = refs[len(names) + len(outs) :]
     variant = flag[0]
-    lefts = jnp.where(variant == 1, lefts_of[1], lefts_of[0])
-    halves = jnp.where(variant == 1, len(parts_of[1]), len(parts_of[0]))
+    lefts = {job[1] for job in jobs}
 
     for which in (0, 1):
 
         @pl.when(variant == which)
         def _(which=which):
-            for slot, part in enumerate(parts_of[which]):
+            for slot, part in parts_of[which].items():
                 name, offset = places[part]
                 pltpu.make_async_copy(
                     sources[name].at[pl.ds(offset, HALF)], blocks.at[slot], sems.at[slot]
                 ).start()
 
-    def squares(slot):
+    def prepare(slot):
         pltpu.make_async_copy(blocks.at[slot], blocks.at[slot], sems.at[slot]).wait()
         values = blocks[slot].astype(jnp.float32)
-        return lane_sums(values * values) * (LOG2E / (2.0 * BAND))
-
-    def prepare_left(slot, carry):
-        norms[slot] = jnp.broadcast_to(
-            jnp.sum(squares(slot), axis=1, keepdims=True), (HALF, LANES)
-        )
-        totals[slot] = jnp.zeros((HALF, LANES), jnp.float32)
-        return carry
-
-    def prepare_right(slot, carry):
-        rights[slot] = as_row(squares(slot))
-        sums[slot] = jnp.zeros((1, HALF), jnp.float32)
-        return carry
-
-    lax.fori_loop(0, lefts, prepare_left, 0)
-    lax.fori_loop(lefts, halves, prepare_right, 0)
-
-    def pair(left, right_slots):
-        for right in right_slots:
-            for at in range(0, HALF, TILE):
-                inner = lax.dot_general(
-                    blocks[left],
-                    blocks[right, at : at + TILE],
-                    (((1,), (1,)), ((), ())),
-                    preferred_element_type=jnp.float32,
+        squares = lane_sums(values * values) * (LOG2E / (2.0 * BAND))
+        if slot in lefts:
+            norms[slot] = jnp.broadcast_to(
+                jnp.sum(squares, axis=1, keepdims=True), (HALF, LANES)
+            )
+        else:
+            rights[slot] = as_row(squares)
+
+    def pair(left, right, seen):
+        for at in range(0, HALF, TILE):
+            inner = lax.dot_general(
+                blocks[left],
+                blocks[right, at : at + TILE],
+                (((1,), (1,)), ((), ())),
+                preferred_element_type=jnp.float32,
+            )
+            rows = None
+            for lane in range(0, TILE, LANES):
+                cut = slice(at + lane, at + lane + LANES)
+                value = jnp.exp2(
+                    inner[:, lane : lane + LANES] * (LOG2E / BAND)
+                    - norms[left]
+                    - rights[right, :, cut]
                 )
-                rows = None
-                for lane in range(0, TILE, LANES):
-                    cut = slice(at + lane, at + lane + LANES)
-                    value = jnp.exp2(
-                        inner[:, lane : lane + LANES] * (LOG2E / BAND)
-                        - norms[left]
-                        - rights[right, :, cut]
-                    )
-                    rows = value if rows is None else rows + value
-                    sums[right, :, cut] += jnp.sum(value, axis=0, keepdims=True)
-                totals[left] += rows
-
-    def double(job, carry):
-        pair(jobs[variant, 3 * job], (jobs[variant, 3 * job + 1], jobs[variant, 3 * job + 2]))
-        return carry
-
-    lax.fori_loop(0, jobs[variant, jobs.shape[1] - 1], double, 0)
-    if has_single:
-        single = jobs.shape[1] - 3
-
-        @pl.when(jobs[variant, single] >= 0)
-        def _():
-            pair(jobs[variant, single], (jobs[variant, single + 1],))
-
-    def finish(slot, carry):
-        sums[slot] = as_row(totals[slot])
-        return carry
-
-    lax.fori_loop(0, lefts, finish, 0)
+                rows = value if rows is None else rows + value
+                column = jnp.sum(value, axis=0, keepdims=True)
+                sums[right, :, cut] = sums[right, :, cut] + column if right in seen else column
+            totals[left] = totals[left] + rows if left in seen else rows
+            seen.add(left)
+        seen.add(right)
+
+    ready, seen = set(), set()
+    for only, left, *right_slots in jobs:
+
+        def work(fresh):
+            for slot in fresh:
+                prepare(slot)
+            for right in right_slots:
+                pair(left, right, seen)
+
+        fresh = [slot for slot in (left, *right_slots) if slot not in ready]
+        ready.update(fresh)
+        if only is None:
+            work(fresh)
+        else:
+            pl.when(variant == only)(functools.partial(work, fresh))
 
     for which in (0, 1):
 
         @pl.when(variant == which)
         def _(which=which):
             for part in outs:
-                if part in parts_of[which]:
-                    results[part][...] = sums[parts_of[which].index(part)]
-                else:
-                    results[part][...] = jnp.zeros_like(results[part])
-
-
-def pair_sums(flag, arrays, jobs_first, jobs_second):
+                found = [slot for slot, other in parts_of[which].items() if other == part]
+                terms = [as_row(totals[i]) if i in lefts else sums[i] for i in found]
+                results[part][...] = sum(terms, jnp.zeros((1, HALF), jnp.float32))
+
+
+def pair_sums(flag, arrays, first_parts, second_parts, jobs):
     names = list(arrays)
     places = {}
     for name in names:
@@ -221,31 +210,17 @@
             places[name] = (name, 0)
         else:
             places[name + "0"], places[name + "1"] = (name, 0), (name, HALF)
-    parts_of, lefts_of, rows = [], [], []
-    lists = (jobs_second, jobs_first)
-    most = max(len(jobs) for jobs in lists)
-    for jobs in lists:
-        left_parts = list(dict.fromkeys(job[0] for job in jobs))
-        right_parts = list(dict.fromkeys(part for job in jobs for part in job[1:]))
-        order = left_parts + right_parts
-        parts_of.append(order)
-        lefts_of.append(len(left_parts))
-        doubles = [job for job in jobs if len(job) == 3]
-        singles = [job for job in jobs if len(job) == 2]
-        row = [order.index(part) for job in doubles for part in job]
-        row += [0] * (3 * most - len(row))
-        row += [order.index(part) for part in singles[0]] if singles else [-1, 0]
-        rows.append(row + [len(doubles)])
-    outs = sorted(set(parts_of[0]) | set(parts_of[1]))
-    slots = max(len(order) for order in parts_of)
-    has_single = any(len(job) == 2 for jobs in lists for job in jobs)
-    smem = pl.BlockSpec(memory_space=pltpu.SMEM)
+    parts_of = [
+        {slot: part for slot, part in enumerate(parts) if part}
+        for parts in (second_parts, first_parts)
+    ]
+    outs = sorted(set(parts_of[0].values()) | set(parts_of[1].values()))
+    slots = len(first_parts)
     results = pl.pallas_call(
-        functools.partial(
-            pairs_kernel, parts_of, lefts_of, names, places, outs, has_single
-        ),
+        functools.partial(pairs_kernel, parts_of, jobs, names, places, outs),
         out_shape=[jax.ShapeDtypeStruct((1, HALF), jnp.float32) for _ in outs],
-        in_specs=[smem, smem] + [pl.BlockSpec(memory_space=pltpu.HBM)] * len(names),
+        in_specs=[pl.BlockSpec(memory_space=pltpu.SMEM)]
+        + [pl.BlockSpec(memory_space=pltpu.HBM)] * len(names),
         out_specs=[pl.BlockSpec(memory_space=pltpu.VMEM)] * len(outs),
         scratch_shapes=[
             pltpu.VMEM((slots, HALF, 1024), jnp.bfloat16),
@@ -257,12 +232,8 @@
         ],
         compiler_params=pltpu.CompilerParams(vmem_limit_bytes=32 * 1024 * 1024),
         cost_estimate=pl.CostEstimate(flops=1, bytes_accessed=1, transcendentals=0),
-    )(flag, jnp.asarray(rows, jnp.int32), *[arrays[name] for name in names])
+    )(flag, *[arrays[name] for name in names])
     return dict(zip(outs, results))
-
-
-def both(lefts, first_right, second_right):
-    return [(left, first_right, second_right) for left in lefts]
 
 
 def whole(first_half, second_half):
@@ -307,8 +278,9 @@
     early = pair_sums(
         flag,
         dict(along=along, one_a=one_a, one_b=one_b),
-        both(["along0", "along1"], "one_a", "one_b"),
-        [],
+        ["along0", "one_a", "one_b", "along1"],
+        [None] * 4,
+        [(1, 0, 1, 2), (1, 3, 1, 2)],
     )
 
     two_a_after = after(two_a, early)
@@ -322,8 +294,9 @@
     middle = pair_sums(
         flag,
         dict(own=own, across=after(across, three_a), two_a=two_a, two_b=two_b, two_c_a=two_c_a),
-        both(["own0", "own1"], "across0", "across1"),
-        both(["across0", "across1", "two_c_a"], "two_a", "two_b"),
+        ["own0", "across0", "across1", "own1", None],
+        ["across0", "two_a", "two_b", "across1", "two_c_a"],
+        [(None, 0, 1, 2), (None, 3, 1, 2), (0, 4, 1, 2)],
     )
     three_c_a = move(three_a, route(three_across))
     late = pair_sums(
@@ -332,8 +305,9 @@
             three_a=three_a, two_a=two_a, two_b=two_b, two_c_b=two_c_b, two_x_a=two_x_a,
             three_c_a=three_c_a,
         ),
-        both(["three_a"], "two_a", "two_b") + [("three_a", "three_c_a")],
-        both(["three_a", "two_c_b"], "two_a", "two_b") + [("three_a", "two_x_a")],
+        ["three_a", "two_a", "two_b", "three_c_a", None],
+        ["three_a", "two_a", "two_b", "two_x_a", "two_c_b"],
+        [(None, 0, 1, 2, 3), (0, 4, 1, 2)],
     )
 
     held = dict(route(own_in_plane))
@@ -356,16 +330,16 @@
             three_b=three_b, two_a=two_a, two_b=two_b, two_x_a=two_x_a, two_x_b=two_x_b,
             three_a=three_a, three_c_a=three_c_a,
         ),
-        both(["three_b"], "two_a", "two_b") + [("three_b", "three_c_a")],
-        both(["three_b"], "two_a", "two_b")
-        + both(["three_b"], "two_x_a", "two_x_b")
-        + [("three_a", "two_x_b")],
+        ["three_b", "two_a", "two_b", "three_c_a", None, None],
+        ["three_b", "two_a", "two_b", "two_x_a", "two_x_b", "three_a"],
+        [(None, 0, 1, 2, 3), (0, 0, 4), (0, 5, 4)],
     )
     final = pair_sums(
         flag,
         dict(three_a=three_a, three_b=three_b, three_c_b=three_c_b),
-        both(["three_c_b"], "three_a", "three_b"),
-        [],
+        ["three_c_b", "three_a", "three_b"],
+        [None] * 3,
+        [(1, 0, 1, 2)],
     )
 
     total = total + whole(middle["own0"], middle["own1"])

time: 123 us -> 118 us (0.959)
  Pallas kernels: 22.8 us -> 17.3 us
    pallas_call x5, Pallas kernels: 22.8 us -> 17.3 us  [pair_sums(): pl.pallas_call(functools.partial(pairs_kernel, parts_of, jobs, names, pla...]
  transfers between devices with their start and end apart: 20 -> 20, of which waited for: 7 -> 7; matrix products, arithmetic and copies ran while one was open for 4% -> 4% of each run, Pallas kernels for 19% -> 15%
where the time goes in v1:
time: 118 us
  waiting for transfers between devices  48.5 us (41%)
  starting transfers between devices  42.9 us (36%)
  Pallas kernels  17.3 us (15%)
  local copies, waits for them, and re-layouts  2.95 us (2%)
  other arithmetic  2.93 us (2%)
  matrix products  2.69 us (2%)
    ppermute x20, waiting for transfers between devices, move(): return lax.ppermute(value, AXES, pairs)  48.5 us
    ppermute x20, starting transfers between devices, move(): return lax.ppermute(value, AXES, pairs)  42.9 us
    pallas_call x5, Pallas kernels, pair_sums(): pl.pallas_call(functools.partial(pairs_kernel, parts_of, jobs, names, pla...  17.3 us
    dot_general x1, matrix products, kernel_block(): lax.dot_general(left, right, (((1,), (1,)), ((), ())), preferred_element_...  2.69 us
  transfers between devices with their start and end apart: 20, of which 7 were waited for; matrix products, arithmetic and copies ran while one was open for 4% of the time, Pallas kernels for 15%

profile of v1, /device:TPU:128, one launch (start us, length us, event | category | flops | bytes accessed | tf_op | source)
XLA Modules:
  0.0 117.7 jit_solution(3819779880779782111)
XLA Ops:
  0.0 1.4 %slice.16 = bf16[512,1024]{1,0:T(8,128)(2,1)S(1)} slice(bf16[1024,1024]{1,0:T(8,128)(2,1)} %refs_0_.1), slice={[0:512], [0:1024]} | slice | bytes 2097152 | tf_op jit(solution)/shard_map/slice | solution.py:256
  1.4 0.5 copy-done
  1.9 1.1 slice.17
  3.0 2.0 %collective-permute-start.1 = (bf16[1024,1024]{1,0:T(8,128)(2,1)S(1)}, bf16[1024,1024]{1,0:T(8,128)(2,1)}, u32[]{:S(2)}, u32[]{:S(2)}) collective-permute-start(bf16[1024,1024]{1,0:T(8,128)(2,1)S(1)} %copy-done), channel_id=1, source_target_pairs={{1,217},{32,96},{33,57},{3,195},{34,98},{5,197},{36,100},{6,14},{7... | collective-permute-start | bytes 6291464 | tf_op jit(solution)/shard_map/ppermute | solution.py:102
  4.9 1.6 %collective-permute-start.2 = (bf16[512,1024]{1,0:T(8,128)(2,1)S(1)}, bf16[512,1024]{1,0:T(8,128)(2,1)}, u32[]{:S(2)}, u32[]{:S(2)}) collective-permute-start(bf16[512,1024]{1,0:T(8,128)(2,1)S(1)} %slice.16), channel_id=1, source_target_pairs={{0,38},{1,33},{32,0},{33,3},{2,32},{3,35},{34,2},{35,5},{4,34},{5,... | collective-permute-start | bytes 3145736 | tf_op jit(solution)/shard_map/ppermute | solution.py:102
  6.5 0.1 collective-permute-start.5
  6.6 2.1 %collective-permute-start = (bf16[1024,1024]{1,0:T(8,128)(2,1)S(1)}, bf16[1024,1024]{1,0:T(8,128)(2,1)}, u32[]{:S(2)}, u32[]{:S(2)}) collective-permute-start(bf16[1024,1024]{1,0:T(8,128)(2,1)S(1)} %copy-done), channel_id=1, source_target_pairs={{0,1},{1,0},{32,57},{33,32},{2,3},{3,10},{34,59},{35,34},{4,5},{5,... | collective-permute-start | bytes 6291464 | tf_op jit(solution)/shard_map/ppermute | solution.py:102
  8.7 0.5 multiply_reduce_fusion
  9.2 11.1 %collective-permute-done.2.refs_1_ = bf16[512,1024]{1,0:T(8,128)(2,1)} collective-permute-done((bf16[512,1024]{1,0:T(8,128)(2,1)S(1)}, bf16[512,1024]{1,0:T(8,128)(2,1)}, u32[]{:S(2)}, u32[]{:S(2)}) %collective-permute-start.2) | collective-permute-done | bytes 1048608 | tf_op jit(solution)/shard_map/ppermute | solution.py:102
  20.3 2.3 %collective-permute-start.3 = (bf16[512,1024]{1,0:T(8,128)(2,1)}, bf16[512,1024]{1,0:T(8,128)(2,1)S(1)}, u32[]{:S(2)}, u32[]{:S(2)}) collective-permute-start(bf16[512,1024]{1,0:T(8,128)(2,1)} %collective-permute-done.2.refs_1_), channel_id=1, source_target_pairs={{0,38},{1,33},{32,0},{33,3},{2,32},{3,59},{34,10},{35,5},{4,34},{5... | collective-permute-start | bytes 3145736 | tf_op jit(solution)/shard_map/ppermute | solution.py:102
  22.7 2.7 %select_reduce_fusion = f32[1024]{0:T(1024)S(1)} fusion(bf16[1024,1024]{1,0:T(8,128)(2,1)S(1)} %copy-done, f32[1024]{0:T(1024)S(1)} %broadcast_multiply_fusion), kind=kOutput, calls=%fused_computation | convolution fusion | flops 2153774080 | bytes 2105344 | tf_op jit(solution)/shard_map/dot_general | solution.py:111
  25.4 6.2 %collective-permute-done.5.refs_2_ = bf16[512,1024]{1,0:T(8,128)(2,1)} collective-permute-done((bf16[512,1024]{1,0:T(8,128)(2,1)}, bf16[512,1024]{1,0:T(8,128)(2,1)}, u32[]{:S(2)}, u32[]{:S(2)}) %collective-permute-start.5) | collective-permute-done | bytes 1048608 | tf_op jit(solution)/shard_map/ppermute | solution.py:102
  31.6 2.3 %collective-permute-start.6 = (bf16[512,1024]{1,0:T(8,128)(2,1)}, bf16[512,1024]{1,0:T(8,128)(2,1)S(1)}, u32[]{:S(2)}, u32[]{:S(2)}) collective-permute-start(bf16[512,1024]{1,0:T(8,128)(2,1)} %collective-permute-done.5.refs_2_), channel_id=1, source_target_pairs={{0,38},{1,33},{32,0},{33,3},{2,32},{3,59},{34,10},{35,5},{4,34},{5... | collective-permute-start | bytes 3145736 | tf_op jit(solution)/shard_map/ppermute | solution.py:102
  33.9 0.0 collective-permute-done.1.refs_0_
  33.9 1.7 %slice_select_fusion = (bf16[512,1024]{1,0:T(8,128)(2,1)S(1)}, bf16[512,1024]{1,0:T(8,128)(2,1)S(1)}) fusion(bf16[1024,1024]{1,0:T(8,128)(2,1)} %collective-permute-done.1.refs_0_, bf16[1024,1024]{1,0:T(8,128)(2,1)S(1)} %copy-done, pred[]{:T(512)S(6)} %or.3), kind=kLoop, calls=%fused_computation.3 | loop fusion | flops 1048576 | bytes 6291457 | tf_op jit(solution)/shard_map/jit(_where)/select_n | solution.py:275
  35.6 0.1 shard_map.17
  35.7 9.5 %collective-permute-done.3.refs_2_.refs_1_ = bf16[512,1024]{1,0:T(8,128)(2,1)S(1)} collective-permute-done((bf16[512,1024]{1,0:T(8,128)(2,1)}, bf16[512,1024]{1,0:T(8,128)(2,1)S(1)}, u32[]{:S(2)}, u32[]{:S(2)}) %collective-permute-start.3) | collective-permute-done | bytes 1048608 | tf_op jit(solution)/shard_map/ppermute | solution.py:102
  45.3 0.0 collective-permute-start.4
  45.3 5.6 %collective-permute-start.11 = (bf16[512,1024]{1,0:T(8,128)(2,1)S(1)}, bf16[512,1024]{1,0:T(8,128)(2,1)S(1)}, u32[]{:S(2)}, u32[]{:S(2)}) collective-permute-start(bf16[512,1024]{1,0:T(8,128)(2,1)S(1)} %collective-permute-done.3.refs_2_.refs_1_), channel_id=1, source_target_pairs={{0,216},{33,105},{2,218},{35,107},{4,220},{37,109},{6,222},{39,111... | collective-permute-start | bytes 3145736 | tf_op jit(solution)/shard_map/ppermute | solution.py:102
  50.8 1.3 %collective-permute-start.7 = (bf16[512,1024]{1,0:T(8,128)(2,1)S(1)}, bf16[512,1024]{1,0:T(8,128)(2,1)S(1)}, u32[]{:S(2)}, u32[]{:S(2)}) collective-permute-start(bf16[512,1024]{1,0:T(8,128)(2,1)S(1)} %collective-permute-done.3.refs_2_.refs_1_), channel_id=1, source_target_pairs={{1,8},{32,57},{3,10},{34,59},{5,12},{36,61},{7,14},{38,63},{9,16},... | collective-permute-start | bytes 3145736 | tf_op jit(solution)/shard_map/ppermute | solution.py:102
  52.1 10.9 %collective-permute-done.6.refs_3_.refs_2_ = bf16[512,1024]{1,0:T(8,128)(2,1)S(1)} collective-permute-done((bf16[512,1024]{1,0:T(8,128)(2,1)}, bf16[512,1024]{1,0:T(8,128)(2,1)S(1)}, u32[]{:S(2)}, u32[]{:S(2)}) %collective-permute-start.6) | collective-permute-done | bytes 1048608 | tf_op jit(solution)/shard_map/ppermute | solution.py:102
  63.0 1.3 %collective-permute-start.10 = (bf16[512,1024]{1,0:T(8,128)(2,1)S(1)}, bf16[512,1024]{1,0:T(8,128)(2,1)S(1)}, u32[]{:S(2)}, u32[]{:S(2)}) collective-permute-start(bf16[512,1024]{1,0:T(8,128)(2,1)S(1)} %collective-permute-done.6.refs_3_.refs_2_), channel_id=1, source_target_pairs={{1,8},{32,57},{3,10},{34,59},{5,12},{36,61},{7,14},{38,63},{9,16},... | collective-permute-start | bytes 3145736 | tf_op jit(solution)/shard_map/ppermute | solution.py:102
  64.3 2.9 %collective-permute-done.4.refs_0_.refs_5_ = bf16[512,1024]{1,0:T(8,128)(2,1)S(1)} collective-permute-done((bf16[512,1024]{1,0:T(8,128)(2,1)S(1)}, bf16[512,1024]{1,0:T(8,128)(2,1)S(1)}, u32[]{:S(2)}, u32[]{:S(2)}) %collective-permute-start.4) | collective-permute-done | bytes 1048608 | tf_op jit(solution)/shard_map/ppermute | solution.py:102
  67.2 1.3 %collective-permute-start.12 = (bf16[512,1024]{1,0:T(8,128)(2,1)S(1)}, bf16[512,1024]{1,0:T(8,128)(2,1)S(1)}, u32[]{:S(2)}, u32[]{:S(2)}) collective-permute-start(bf16[512,1024]{1,0:T(8,128)(2,1)S(1)} %collective-permute-done.4.refs_0_.refs_5_), channel_id=1, source_target_pairs={{0,1},{33,32},{2,3},{35,34},{4,5},{37,36},{6,7},{39,38},{8,9},{41,... | collective-permute-start | bytes 3145736 | tf_op jit(solution)/shard_map/ppermute | solution.py:102
  68.6 0.0 collective-permute-done.11.refs_4_.refs_3_
  68.6 1.7 %collective-permute-start.13 = (bf16[512,1024]{1,0:T(8,128)(2,1)S(1)}, bf16[512,1024]{1,0:T(8,128)(2,1)S(1)}, u32[]{:S(2)}, u32[]{:S(2)}) collective-permute-start(bf16[512,1024]{1,0:T(8,128)(2,1)S(1)} %get-tuple-element.62), channel_id=1, source_target_pairs={{0,32},{1,39},{32,2},{33,1},{2,34},{3,33},{34,4},{35,3},{4,36},{5,... | collective-permute-start | bytes 3145736 | tf_op jit(solution)/shard_map/ppermute | solution.py:102
  70.3 0.0 collective-permute-done.refs_1_
  70.3 6.5 %collective-permute-start.14 = (bf16[512,1024]{1,0:T(8,128)(2,1)S(1)}, bf16[512,1024]{1,0:T(8,128)(2,1)S(1)}, u32[]{:S(2)}, u32[]{:S(2)}) collective-permute-start(bf16[512,1024]{1,0:T(8,128)(2,1)S(1)} %collective-permute-done.6.refs_3_.refs_2_), channel_id=1, source_target_pairs={{0,216},{33,105},{2,218},{35,107},{4,220},{37,109},{6,222},{39,111... | collective-permute-start | bytes 3145736 | tf_op jit(solution)/shard_map/ppermute | solution.py:102
  76.8 0.0 collective-permute-done.7.refs_4_
  76.8 0.7 collective-permute-start.8
  77.5 6.5 %shard_map.18 = (f32[1,512]{1,0:T(1,128)S(1)}, f32[1,512]{1,0:T(1,128)S(1)}, f32[1,512]{1,0:T(1,128)S(1)}, f32[1,512]{1,0:T(1,128)S(1)}, f32[1,512]{1,0:T(1,128)...) custom-call(s32[1]{0:T(128)} %bitcast.flag, bf16[1024,1024]{1,0:T(8,128)(2,1)S(1)} %copy-done, ...), custom_call_target="tpu_custom_call" | custom-call | flops 1 | bytes 1 | tf_op jit(solution)/shard_map/pallas_call | solution.py:219
  84.0 0.0 collective-permute-done.10.refs_3_
  84.0 0.1 collective-permute-start.9
  84.1 0.0 collective-permute-done.12.refs_5_.refs_6_
  84.1 5.1 %shard_map.19 = (f32[1,512]{1,0:T(1,128)S(1)}, f32[1,512]{1,0:T(1,128)S(1)}, f32[1,512]{1,0:T(1,128)S(1)}, f32[1,512]{1,0:T(1,128)S(1)}, f32[1,512]{1,0:T(1,128)S(1)}, /*index=5*/f32[1,512]{1,0:T(1,128)S(1)}) custom-call(s32[1]{0:T(128)} %bitcast.flag, bf16[512,1024]{1,0:T(8,128)(2,1)S(1)} %collective-permute-done.4.refs_0_.refs_5_, ...), custom_call_target="tpu_custom_call" | custom-call | flops 1 | bytes 1 | tf_op jit(solution)/shard_map/pallas_call | solution.py:219
  89.2 0.0 collective-permute-done.8
  89.2 0.0 collective-permute-done.13.refs_0_.refs_1_
  89.3 0.0 collective-permute-done.9
  89.3 1.4 %collective-permute-start.17 = (bf16[512,1024]{1,0:T(8,128)(2,1)S(1)}, bf16[512,1024]{1,0:T(8,128)(2,1)S(1)}, u32[]{:S(2)}, u32[]{:S(2)}) collective-permute-start(bf16[512,1024]{1,0:T(8,128)(2,1)S(1)} %collective-permute-done.13.refs_0_.refs_1_), channel_id=1, source_target_pairs={{0,1},{33,32},{2,3},{35,34},{4,5},{37,36},{6,7},{39,38},{8,9},{41,... | collective-permute-start | bytes 3145736 | tf_op jit(solution)/shard_map/ppermute | solution.py:102
  90.6 0.0 collective-permute-done.14.refs_4_
  90.7 5.6 %shard_map.20 = (f32[1,512]{1,0:T(1,128)S(1)}, f32[1,512]{1,0:T(1,128)S(1)}, f32[1,512]{1,0:T(1,128)S(1)}, f32[1,512]{1,0:T(1,128)S(1)}, f32[1,512]{1,0:T(1,128)...) custom-call(s32[1]{0:T(128)} %bitcast.flag, bf16[512,1024]{1,0:T(8,128)(2,1)S(1)} %collective-permute-done.13.refs_0_.refs_1_, ...), custom_call_target="tpu_custom_call" | custom-call | flops 1 | bytes 1 | tf_op jit(solution)/shard_map/pallas_call | solution.py:219
  96.3 0.1 collective-permute-start.15
  96.4 6.4 %collective-permute-start.16 = (f32[1024]{0:T(1024)S(1)}, f32[1024]{0:T(1024)S(1)}, u32[]{:S(2)}, u32[]{:S(2)}) collective-permute-start(f32[1024]{0:T(1024)S(1)} %pad_maximum_fusion.3), channel_id=1, source_target_pairs={{6,0},{3,1},{38,32},{59,33},{0,2},{5,3},{32,34},{61,35},{10,4},{7,... | collective-permute-start | bytes 12296 | tf_op jit(solution)/shard_map/ppermute | solution.py:102
  102.9 6.2 %collective-permute-start.18 = (f32[1024]{0:T(1024)S(1)}, f32[1024]{0:T(1024)S(1)}, u32[]{:S(2)}, u32[]{:S(2)}) collective-permute-start(f32[1024]{0:T(1024)S(1)} %pad_maximum_fusion.4), channel_id=1, source_target_pairs={{32,0},{39,1},{2,32},{25,33},{34,2},{33,3},{4,34},{3,35},{36,4},{3... | collective-permute-start | bytes 12296 | tf_op jit(solution)/shard_map/ppermute | solution.py:102
  109.1 0.1 collective-permute-start.19
  109.3 1.2 %collective-permute-done.18 = f32[1024]{0:T(1024)S(1)} collective-permute-done((f32[1024]{0:T(1024)S(1)}, f32[1024]{0:T(1024)S(1)}, u32[]{:S(2)}, u32[]{:S(2)}) %collective-permute-start.18) | collective-permute-done | bytes 4128 | tf_op jit(solution)/shard_map/ppermute | solution.py:102
  110.5 6.6 %collective-permute-done.19 = f32[1024]{0:T(1024)S(1)} collective-permute-done((f32[1024]{0:T(1024)S(1)}, f32[1024]{0:T(1024)S(1)}, u32[]{:S(2)}, u32[]{:S(2)}) %collective-permute-start.19) | collective-permute-done | bytes 4128 | tf_op jit(solution)/shard_map/ppermute | solution.py:102
  117.0 0.6 fusion.7
  (18 shorter events, 0.1 us)
Async XLA Ops:
  0.0 1.9 %copy-start = (bf16[1024,1024]{1,0:T(8,128)(2,1)S(1)}, bf16[1024,1024]{1,0:T(8,128)(2,1)}, u32[]{:S(2)}) copy-start(bf16[1024,1024]{1,0:T(8,128)(2,1)} %refs_0_.1) | copy-start | bytes 6291460
  3.0 30.9 %collective-permute-start.1 = (bf16[1024,1024]{1,0:T(8,128)(2,1)S(1)}, bf16[1024,1024]{1,0:T(8,128)(2,1)}, u32[]{:S(2)}, u32[]{:S(2)}) collective-permute-start(bf16[1024,1024]{1,0:T(8,128)(2,1)S(1)} %copy-done), channel_id=1, source_target_pairs={{1,217},{32,96},{33,57},{3,195},{34,98},{5,197},{36,100},{6,14},{7... | collective-permute-start | bytes 6291464 | tf_op jit(solution)/shard_map/ppermute | solution.py:102
  4.9 15.4 %collective-permute-start.2 = (bf16[512,1024]{1,0:T(8,128)(2,1)S(1)}, bf16[512,1024]{1,0:T(8,128)(2,1)}, u32[]{:S(2)}, u32[]{:S(2)}) collective-permute-start(bf16[512,1024]{1,0:T(8,128)(2,1)S(1)} %slice.16), channel_id=1, source_target_pairs={{0,38},{1,33},{32,0},{33,3},{2,32},{3,35},{34,2},{35,5},{4,34},{5,... | collective-permute-start | bytes 3145736 | tf_op jit(solution)/shard_map/ppermute | solution.py:102
  6.5 25.0 %collective-permute-start.5 = (bf16[512,1024]{1,0:T(8,128)(2,1)}, bf16[512,1024]{1,0:T(8,128)(2,1)}, u32[]{:S(2)}, u32[]{:S(2)}) collective-permute-start(bf16[512,1024]{1,0:T(8,128)(2,1)} %slice.17), channel_id=1, source_target_pairs={{0,38},{1,33},{32,0},{33,3},{2,32},{3,35},{34,2},{35,5},{4,34},{5,... | collective-permute-start | bytes 3145736 | tf_op jit(solution)/shard_map/ppermute | solution.py:102
  6.6 63.7 %collective-permute-start = (bf16[1024,1024]{1,0:T(8,128)(2,1)S(1)}, bf16[1024,1024]{1,0:T(8,128)(2,1)}, u32[]{:S(2)}, u32[]{:S(2)}) collective-permute-start(bf16[1024,1024]{1,0:T(8,128)(2,1)S(1)} %copy-done), channel_id=1, source_target_pairs={{0,1},{1,0},{32,57},{33,32},{2,3},{3,10},{34,59},{35,34},{4,5},{5,... | collective-permute-start | bytes 6291464 | tf_op jit(solution)/shard_map/ppermute | solution.py:102
  20.3 24.9 %collective-permute-start.3 = (bf16[512,1024]{1,0:T(8,128)(2,1)}, bf16[512,1024]{1,0:T(8,128)(2,1)S(1)}, u32[]{:S(2)}, u32[]{:S(2)}) collective-permute-start(bf16[512,1024]{1,0:T(8,128)(2,1)} %collective-permute-done.2.refs_1_), channel_id=1, source_target_pairs={{0,38},{1,33},{32,0},{33,3},{2,32},{3,59},{34,10},{35,5},{4,34},{5... | collective-permute-start | bytes 3145736 | tf_op jit(solution)/shard_map/ppermute | solution.py:102
  31.6 31.5 %collective-permute-start.6 = (bf16[512,1024]{1,0:T(8,128)(2,1)}, bf16[512,1024]{1,0:T(8,128)(2,1)S(1)}, u32[]{:S(2)}, u32[]{:S(2)}) collective-permute-start(bf16[512,1024]{1,0:T(8,128)(2,1)} %collective-permute-done.5.refs_2_), channel_id=1, source_target_pairs={{0,38},{1,33},{32,0},{33,3},{2,32},{3,59},{34,10},{35,5},{4,34},{5... | collective-permute-start | bytes 3145736 | tf_op jit(solution)/shard_map/ppermute | solution.py:102
  45.3 22.0 %collective-permute-start.4 = (bf16[512,1024]{1,0:T(8,128)(2,1)S(1)}, bf16[512,1024]{1,0:T(8,128)(2,1)S(1)}, u32[]{:S(2)}, u32[]{:S(2)}) collective-permute-start(bf16[512,1024]{1,0:T(8,128)(2,1)S(1)} %get-tuple-element.47), channel_id=1, source_target_pairs={{0,32},{1,39},{32,2},{33,1},{2,34},{3,33},{34,4},{35,3},{4,36},{5,... | collective-permute-start | bytes 3145736 | tf_op jit(solution)/shard_map/ppermute | solution.py:102
  45.3 23.3 %collective-permute-start.11 = (bf16[512,1024]{1,0:T(8,128)(2,1)S(1)}, bf16[512,1024]{1,0:T(8,128)(2,1)S(1)}, u32[]{:S(2)}, u32[]{:S(2)}) collective-permute-start(bf16[512,1024]{1,0:T(8,128)(2,1)S(1)} %collective-permute-done.3.refs_2_.refs_1_), channel_id=1, source_target_pairs={{0,216},{33,105},{2,218},{35,107},{4,220},{37,109},{6,222},{39,111... | collective-permute-start | bytes 3145736 | tf_op jit(solution)/shard_map/ppermute | solution.py:102
  50.8 26.0 %collective-permute-start.7 = (bf16[512,1024]{1,0:T(8,128)(2,1)S(1)}, bf16[512,1024]{1,0:T(8,128)(2,1)S(1)}, u32[]{:S(2)}, u32[]{:S(2)}) collective-permute-start(bf16[512,1024]{1,0:T(8,128)(2,1)S(1)} %collective-permute-done.3.refs_2_.refs_1_), channel_id=1, source_target_pairs={{1,8},{32,57},{3,10},{34,59},{5,12},{36,61},{7,14},{38,63},{9,16},... | collective-permute-start | bytes 3145736 | tf_op jit(solution)/shard_map/ppermute | solution.py:102
  63.0 21.0 %collective-permute-start.10 = (bf16[512,1024]{1,0:T(8,128)(2,1)S(1)}, bf16[512,1024]{1,0:T(8,128)(2,1)S(1)}, u32[]{:S(2)}, u32[]{:S(2)}) collective-permute-start(bf16[512,1024]{1,0:T(8,128)(2,1)S(1)} %collective-permute-done.6.refs_3_.refs_2_), channel_id=1, source_target_pairs={{1,8},{32,57},{3,10},{34,59},{5,12},{36,61},{7,14},{38,63},{9,16},... | collective-permute-start | bytes 3145736 | tf_op jit(solution)/shard_map/ppermute | solution.py:102
  67.2 16.9 %collective-permute-start.12 = (bf16[512,1024]{1,0:T(8,128)(2,1)S(1)}, bf16[512,1024]{1,0:T(8,128)(2,1)S(1)}, u32[]{:S(2)}, u32[]{:S(2)}) collective-permute-start(bf16[512,1024]{1,0:T(8,128)(2,1)S(1)} %collective-permute-done.4.refs_0_.refs_5_), channel_id=1, source_target_pairs={{0,1},{33,32},{2,3},{35,34},{4,5},{37,36},{6,7},{39,38},{8,9},{41,... | collective-permute-start | bytes 3145736 | tf_op jit(solution)/shard_map/ppermute | solution.py:102
  68.6 20.6 %collective-permute-start.13 = (bf16[512,1024]{1,0:T(8,128)(2,1)S(1)}, bf16[512,1024]{1,0:T(8,128)(2,1)S(1)}, u32[]{:S(2)}, u32[]{:S(2)}) collective-permute-start(bf16[512,1024]{1,0:T(8,128)(2,1)S(1)} %get-tuple-element.62), channel_id=1, source_target_pairs={{0,32},{1,39},{32,2},{33,1},{2,34},{3,33},{34,4},{35,3},{4,36},{5,... | collective-permute-start | bytes 3145736 | tf_op jit(solution)/shard_map/ppermute | solution.py:102
  70.3 20.3 %collective-permute-start.14 = (bf16[512,1024]{1,0:T(8,128)(2,1)S(1)}, bf16[512,1024]{1,0:T(8,128)(2,1)S(1)}, u32[]{:S(2)}, u32[]{:S(2)}) collective-permute-start(bf16[512,1024]{1,0:T(8,128)(2,1)S(1)} %collective-permute-done.6.refs_3_.refs_2_), channel_id=1, source_target_pairs={{0,216},{33,105},{2,218},{35,107},{4,220},{37,109},{6,222},{39,111... | collective-permute-start | bytes 3145736 | tf_op jit(solution)/shard_map/ppermute | solution.py:102
  76.8 12.4 %collective-permute-start.8 = (f32[1024]{0:T(1024)S(1)}, f32[1024]{0:T(1024)S(1)}, u32[]{:S(2)}, u32[]{:S(2)}) collective-permute-start(f32[1024]{0:T(1024)S(1)} %pad_maximum_fusion), channel_id=1, source_target_pairs={{217,1},{96,32},{195,3},{98,34},{197,5},{100,36},{199,7},{110,38},... | collective-permute-start | bytes 12296 | tf_op jit(solution)/shard_map/ppermute | solution.py:102
  84.0 5.2 %collective-permute-start.9 = (f32[1024]{0:T(1024)S(1)}, f32[1024]{0:T(1024)S(1)}, u32[]{:S(2)}, u32[]{:S(2)}) collective-permute-start(f32[1024]{0:T(1024)S(1)} %pad_maximum_fusion.1), channel_id=1, source_target_pairs={{1,0},{0,1},{57,32},{32,33},{3,2},{10,3},{59,34},{34,35},{5,4},{12... | collective-permute-start | bytes 12296 | tf_op jit(solution)/shard_map/ppermute | solution.py:102
  89.3 13.6 %collective-permute-start.17 = (bf16[512,1024]{1,0:T(8,128)(2,1)S(1)}, bf16[512,1024]{1,0:T(8,128)(2,1)S(1)}, u32[]{:S(2)}, u32[]{:S(2)}) collective-permute-start(bf16[512,1024]{1,0:T(8,128)(2,1)S(1)} %collective-permute-done.13.refs_0_.refs_1_), channel_id=1, source_target_pairs={{0,1},{33,32},{2,3},{35,34},{4,5},{37,36},{6,7},{39,38},{8,9},{41,... | collective-permute-start | bytes 3145736 | tf_op jit(solution)/shard_map/ppermute | solution.py:102
  96.3 12.9 %collective-permute-start.15 = (f32[1024]{0:T(1024)S(1)}, f32[1024]{0:T(1024)S(1)}, u32[]{:S(2)}, u32[]{:S(2)}) collective-permute-start(f32[1024]{0:T(1024)S(1)} %pad_maximum_fusion.2), channel_id=1, source_target_pairs={{38,0},{3,33},{32,2},{5,35},{34,4},{7,37},{36,6},{1,39},{46,8},{11... | collective-permute-start | bytes 12296 | tf_op jit(solution)/shard_map/ppermute | solution.py:102
  96.4 12.8 %collective-permute-start.16 = (f32[1024]{0:T(1024)S(1)}, f32[1024]{0:T(1024)S(1)}, u32[]{:S(2)}, u32[]{:S(2)}) collective-permute-start(f32[1024]{0:T(1024)S(1)} %pad_maximum_fusion.3), channel_id=1, source_target_pairs={{6,0},{3,1},{38,32},{59,33},{0,2},{5,3},{32,34},{61,35},{10,4},{7,... | collective-permute-start | bytes 12296 | tf_op jit(solution)/shard_map/ppermute | solution.py:102
  102.9 7.5 %collective-permute-start.18 = (f32[1024]{0:T(1024)S(1)}, f32[1024]{0:T(1024)S(1)}, u32[]{:S(2)}, u32[]{:S(2)}) collective-permute-start(f32[1024]{0:T(1024)S(1)} %pad_maximum_fusion.4), channel_id=1, source_target_pairs={{32,0},{39,1},{2,32},{25,33},{34,2},{33,3},{4,34},{3,35},{36,4},{3... | collective-permute-start | bytes 12296 | tf_op jit(solution)/shard_map/ppermute | solution.py:102
  109.1 7.9 %collective-permute-start.19 = (f32[1024]{0:T(1024)S(1)}, f32[1024]{0:T(1024)S(1)}, u32[]{:S(2)}, u32[]{:S(2)}) collective-permute-start(f32[1024]{0:T(1024)S(1)} %pad_maximum_fusion.5), channel_id=1, source_target_pairs={{38,1},{3,32},{32,3},{5,34},{34,5},{7,36},{36,7},{1,38},{46,9},{11... | collective-permute-start | bytes 12296 | tf_op jit(solution)/shard_map/ppermute | solution.py:102

commit v2 on v1

--- a/solution.py
+++ b/solution.py
@@ -345,9 +345,7 @@
     total = total + whole(middle["own0"], middle["own1"])
     total = total + along_sums + across_sums
     total = total + move(
-        after(
-            whole(early["one_a"] + middle["two_c_a"], early["one_b"] + late["two_c_b"]), last
-        ),
+        whole(early["one_a"] + middle["two_c_a"], early["one_b"] + late["two_c_b"]),
         back(one_pairs + route(hop_one, hop_two, two_across)),
     )
     total = total + move(

time: 118 us -> 116 us (0.983)
  starting transfers between devices: 42.9 us -> 41 us
    ppermute x20, starting transfers between devices: 42.9 us -> 41 us  [move(): return lax.ppermute(value, AXES, pairs)]
where the time goes in v2:
time: 116 us
  waiting for transfers between devices  48.5 us (42%)
  starting transfers between devices  41 us (35%)
  Pallas kernels  17.3 us (15%)
  local copies, waits for them, and re-layouts  2.95 us (3%)
  other arithmetic  2.93 us (3%)
  matrix products  2.69 us (2%)
    ppermute x20, waiting for transfers between devices, move(): return lax.ppermute(value, AXES, pairs)  48.5 us
    ppermute x20, starting transfers between devices, move(): return lax.ppermute(value, AXES, pairs)  41 us
    pallas_call x5, Pallas kernels, pair_sums(): pl.pallas_call(functools.partial(pairs_kernel, parts_of, jobs, names, pla...  17.3 us
    dot_general x1, matrix products, kernel_block(): lax.dot_general(left, right, (((1,), (1,)), ((), ())), preferred_element_...  2.69 us
  transfers between devices with their start and end apart: 20, of which 7 were waited for; matrix products, arithmetic and copies ran while one was open for 4% of the time, Pallas kernels for 15%

profile of v2, /device:TPU:128, one launch (start us, length us, event | category | flops | bytes accessed | tf_op | source)
XLA Modules:
  0.0 115.8 jit_solution(18193021943132352943)
XLA Ops:
  0.0 1.4 %slice.16 = bf16[512,1024]{1,0:T(8,128)(2,1)S(1)} slice(bf16[1024,1024]{1,0:T(8,128)(2,1)} %refs_0_.1), slice={[0:512], [0:1024]} | slice | bytes 2097152 | tf_op jit(solution)/shard_map/slice | solution.py:256
  1.4 0.5 copy-done
  1.9 1.1 slice.17
  3.0 2.0 %collective-permute-start.1 = (bf16[1024,1024]{1,0:T(8,128)(2,1)S(1)}, bf16[1024,1024]{1,0:T(8,128)(2,1)}, u32[]{:S(2)}, u32[]{:S(2)}) collective-permute-start(bf16[1024,1024]{1,0:T(8,128)(2,1)S(1)} %copy-done), channel_id=1, source_target_pairs={{1,217},{32,96},{33,57},{3,195},{34,98},{5,197},{36,100},{6,14},{7... | collective-permute-start | bytes 6291464 | tf_op jit(solution)/shard_map/ppermute | solution.py:102
  4.9 1.6 %collective-permute-start.2 = (bf16[512,1024]{1,0:T(8,128)(2,1)S(1)}, bf16[512,1024]{1,0:T(8,128)(2,1)}, u32[]{:S(2)}, u32[]{:S(2)}) collective-permute-start(bf16[512,1024]{1,0:T(8,128)(2,1)S(1)} %slice.16), channel_id=1, source_target_pairs={{0,38},{1,33},{32,0},{33,3},{2,32},{3,35},{34,2},{35,5},{4,34},{5,... | collective-permute-start | bytes 3145736 | tf_op jit(solution)/shard_map/ppermute | solution.py:102
  6.5 0.1 collective-permute-start.5
  6.6 2.1 %collective-permute-start = (bf16[1024,1024]{1,0:T(8,128)(2,1)S(1)}, bf16[1024,1024]{1,0:T(8,128)(2,1)}, u32[]{:S(2)}, u32[]{:S(2)}) collective-permute-start(bf16[1024,1024]{1,0:T(8,128)(2,1)S(1)} %copy-done), channel_id=1, source_target_pairs={{0,1},{1,0},{32,57},{33,32},{2,3},{3,10},{34,59},{35,34},{4,5},{5,... | collective-permute-start | bytes 6291464 | tf_op jit(solution)/shard_map/ppermute | solution.py:102
  8.7 0.5 multiply_reduce_fusion
  9.2 11.1 %collective-permute-done.2.refs_1_ = bf16[512,1024]{1,0:T(8,128)(2,1)} collective-permute-done((bf16[512,1024]{1,0:T(8,128)(2,1)S(1)}, bf16[512,1024]{1,0:T(8,128)(2,1)}, u32[]{:S(2)}, u32[]{:S(2)}) %collective-permute-start.2) | collective-permute-done | bytes 1048608 | tf_op jit(solution)/shard_map/ppermute | solution.py:102
  20.3 2.3 %collective-permute-start.3 = (bf16[512,1024]{1,0:T(8,128)(2,1)}, bf16[512,1024]{1,0:T(8,128)(2,1)S(1)}, u32[]{:S(2)}, u32[]{:S(2)}) collective-permute-start(bf16[512,1024]{1,0:T(8,128)(2,1)} %collective-permute-done.2.refs_1_), channel_id=1, source_target_pairs={{0,38},{1,33},{32,0},{33,3},{2,32},{3,59},{34,10},{35,5},{4,34},{5... | collective-permute-start | bytes 3145736 | tf_op jit(solution)/shard_map/ppermute | solution.py:102
  22.7 2.7 %select_reduce_fusion = f32[1024]{0:T(1024)S(1)} fusion(bf16[1024,1024]{1,0:T(8,128)(2,1)S(1)} %copy-done, f32[1024]{0:T(1024)S(1)} %broadcast_multiply_fusion), kind=kOutput, calls=%fused_computation | convolution fusion | flops 2153774080 | bytes 2105344 | tf_op jit(solution)/shard_map/dot_general | solution.py:111
  25.4 6.2 %collective-permute-done.5.refs_2_ = bf16[512,1024]{1,0:T(8,128)(2,1)} collective-permute-done((bf16[512,1024]{1,0:T(8,128)(2,1)}, bf16[512,1024]{1,0:T(8,128)(2,1)}, u32[]{:S(2)}, u32[]{:S(2)}) %collective-permute-start.5) | collective-permute-done | bytes 1048608 | tf_op jit(solution)/shard_map/ppermute | solution.py:102
  31.6 2.3 %collective-permute-start.6 = (bf16[512,1024]{1,0:T(8,128)(2,1)}, bf16[512,1024]{1,0:T(8,128)(2,1)S(1)}, u32[]{:S(2)}, u32[]{:S(2)}) collective-permute-start(bf16[512,1024]{1,0:T(8,128)(2,1)} %collective-permute-done.5.refs_2_), channel_id=1, source_target_pairs={{0,38},{1,33},{32,0},{33,3},{2,32},{3,59},{34,10},{35,5},{4,34},{5... | collective-permute-start | bytes 3145736 | tf_op jit(solution)/shard_map/ppermute | solution.py:102
  33.9 0.0 collective-permute-done.1.refs_0_
  33.9 1.7 %slice_select_fusion = (bf16[512,1024]{1,0:T(8,128)(2,1)S(1)}, bf16[512,1024]{1,0:T(8,128)(2,1)S(1)}) fusion(bf16[1024,1024]{1,0:T(8,128)(2,1)} %collective-permute-done.1.refs_0_, bf16[1024,1024]{1,0:T(8,128)(2,1)S(1)} %copy-done, pred[]{:T(512)S(6)} %or.3), kind=kLoop, calls=%fused_computation.3 | loop fusion | flops 1048576 | bytes 6291457 | tf_op jit(solution)/shard_map/jit(_where)/select_n | solution.py:275
  35.6 0.1 shard_map.17
  35.7 9.5 %collective-permute-done.3.refs_2_.refs_1_ = bf16[512,1024]{1,0:T(8,128)(2,1)S(1)} collective-permute-done((bf16[512,1024]{1,0:T(8,128)(2,1)}, bf16[512,1024]{1,0:T(8,128)(2,1)S(1)}, u32[]{:S(2)}, u32[]{:S(2)}) %collective-permute-start.3) | collective-permute-done | bytes 1048608 | tf_op jit(solution)/shard_map/ppermute | solution.py:102
  45.3 0.0 collective-permute-start.4
  45.3 5.6 %collective-permute-start.11 = (bf16[512,1024]{1,0:T(8,128)(2,1)S(1)}, bf16[512,1024]{1,0:T(8,128)(2,1)S(1)}, u32[]{:S(2)}, u32[]{:S(2)}) collective-permute-start(bf16[512,1024]{1,0:T(8,128)(2,1)S(1)} %collective-permute-done.3.refs_2_.refs_1_), channel_id=1, source_target_pairs={{0,216},{33,105},{2,218},{35,107},{4,220},{37,109},{6,222},{39,111... | collective-permute-start | bytes 3145736 | tf_op jit(solution)/shard_map/ppermute | solution.py:102
  50.8 1.3 %collective-permute-start.7 = (bf16[512,1024]{1,0:T(8,128)(2,1)S(1)}, bf16[512,1024]{1,0:T(8,128)(2,1)S(1)}, u32[]{:S(2)}, u32[]{:S(2)}) collective-permute-start(bf16[512,1024]{1,0:T(8,128)(2,1)S(1)} %collective-permute-done.3.refs_2_.refs_1_), channel_id=1, source_target_pairs={{1,8},{32,57},{3,10},{34,59},{5,12},{36,61},{7,14},{38,63},{9,16},... | collective-permute-start | bytes 3145736 | tf_op jit(solution)/shard_map/ppermute | solution.py:102
  52.1 10.9 %collective-permute-done.6.refs_3_.refs_2_ = bf16[512,1024]{1,0:T(8,128)(2,1)S(1)} collective-permute-done((bf16[512,1024]{1,0:T(8,128)(2,1)}, bf16[512,1024]{1,0:T(8,128)(2,1)S(1)}, u32[]{:S(2)}, u32[]{:S(2)}) %collective-permute-start.6) | collective-permute-done | bytes 1048608 | tf_op jit(solution)/shard_map/ppermute | solution.py:102
  63.0 1.3 %collective-permute-start.10 = (bf16[512,1024]{1,0:T(8,128)(2,1)S(1)}, bf16[512,1024]{1,0:T(8,128)(2,1)S(1)}, u32[]{:S(2)}, u32[]{:S(2)}) collective-permute-start(bf16[512,1024]{1,0:T(8,128)(2,1)S(1)} %collective-permute-done.6.refs_3_.refs_2_), channel_id=1, source_target_pairs={{1,8},{32,57},{3,10},{34,59},{5,12},{36,61},{7,14},{38,63},{9,16},... | collective-permute-start | bytes 3145736 | tf_op jit(solution)/shard_map/ppermute | solution.py:102
  64.3 2.9 %collective-permute-done.4.refs_0_.refs_5_ = bf16[512,1024]{1,0:T(8,128)(2,1)S(1)} collective-permute-done((bf16[512,1024]{1,0:T(8,128)(2,1)S(1)}, bf16[512,1024]{1,0:T(8,128)(2,1)S(1)}, u32[]{:S(2)}, u32[]{:S(2)}) %collective-permute-start.4) | collective-permute-done | bytes 1048608 | tf_op jit(solution)/shard_map/ppermute | solution.py:102
  67.2 1.3 %collective-permute-start.12 = (bf16[512,1024]{1,0:T(8,128)(2,1)S(1)}, bf16[512,1024]{1,0:T(8,128)(2,1)S(1)}, u32[]{:S(2)}, u32[]{:S(2)}) collective-permute-start(bf16[512,1024]{1,0:T(8,128)(2,1)S(1)} %collective-permute-done.4.refs_0_.refs_5_), channel_id=1, source_target_pairs={{0,1},{33,32},{2,3},{35,34},{4,5},{37,36},{6,7},{39,38},{8,9},{41,... | collective-permute-start | bytes 3145736 | tf_op jit(solution)/shard_map/ppermute | solution.py:102
  68.6 0.0 collective-permute-done.11.refs_4_.refs_3_
  68.6 1.7 %collective-permute-start.14 = (bf16[512,1024]{1,0:T(8,128)(2,1)S(1)}, bf16[512,1024]{1,0:T(8,128)(2,1)S(1)}, u32[]{:S(2)}, u32[]{:S(2)}) collective-permute-start(bf16[512,1024]{1,0:T(8,128)(2,1)S(1)} %get-tuple-element.63), channel_id=1, source_target_pairs={{0,32},{1,39},{32,2},{33,1},{2,34},{3,33},{34,4},{35,3},{4,36},{5,... | collective-permute-start | bytes 3145736 | tf_op jit(solution)/shard_map/ppermute | solution.py:102
  70.3 0.0 collective-permute-done.refs_1_
  70.3 6.5 %collective-permute-start.15 = (bf16[512,1024]{1,0:T(8,128)(2,1)S(1)}, bf16[512,1024]{1,0:T(8,128)(2,1)S(1)}, u32[]{:S(2)}, u32[]{:S(2)}) collective-permute-start(bf16[512,1024]{1,0:T(8,128)(2,1)S(1)} %collective-permute-done.6.refs_3_.refs_2_), channel_id=1, source_target_pairs={{0,216},{33,105},{2,218},{35,107},{4,220},{37,109},{6,222},{39,111... | collective-permute-start | bytes 3145736 | tf_op jit(solution)/shard_map/ppermute | solution.py:102
  76.8 0.0 collective-permute-done.7.refs_4_
  76.8 0.7 collective-permute-start.8
  77.5 6.5 %shard_map.18 = (f32[1,512]{1,0:T(1,128)S(1)}, f32[1,512]{1,0:T(1,128)S(1)}, f32[1,512]{1,0:T(1,128)S(1)}, f32[1,512]{1,0:T(1,128)S(1)}, f32[1,512]{1,0:T(1,128)...) custom-call(s32[1]{0:T(128)} %bitcast.flag, bf16[1024,1024]{1,0:T(8,128)(2,1)S(1)} %copy-done, ...), custom_call_target="tpu_custom_call" | custom-call | flops 1 | bytes 1 | tf_op jit(solution)/shard_map/pallas_call | solution.py:219
  84.0 0.0 collective-permute-done.10.refs_3_
  84.0 0.1 collective-permute-start.9
  84.1 5.1 %shard_map.19 = (f32[1,512]{1,0:T(1,128)S(1)}, f32[1,512]{1,0:T(1,128)S(1)}, f32[1,512]{1,0:T(1,128)S(1)}, f32[1,512]{1,0:T(1,128)S(1)}, f32[1,512]{1,0:T(1,128)S(1)}, /*index=5*/f32[1,512]{1,0:T(1,128)S(1)}) custom-call(s32[1]{0:T(128)} %bitcast.flag, bf16[512,1024]{1,0:T(8,128)(2,1)S(1)} %collective-permute-done.4.refs_0_.refs_5_, ...), custom_call_target="tpu_custom_call" | custom-call | flops 1 | bytes 1 | tf_op jit(solution)/shard_map/pallas_call | solution.py:219
  89.2 0.0 collective-permute-done.14.refs_0_.refs_1_
  89.3 0.0 collective-permute-done.9
  89.3 1.4 %collective-permute-start.17 = (bf16[512,1024]{1,0:T(8,128)(2,1)S(1)}, bf16[512,1024]{1,0:T(8,128)(2,1)S(1)}, u32[]{:S(2)}, u32[]{:S(2)}) collective-permute-start(bf16[512,1024]{1,0:T(8,128)(2,1)S(1)} %collective-permute-done.14.refs_0_.refs_1_), channel_id=1, source_target_pairs={{0,1},{33,32},{2,3},{35,34},{4,5},{37,36},{6,7},{39,38},{8,9},{41,... | collective-permute-start | bytes 3145736 | tf_op jit(solution)/shard_map/ppermute | solution.py:102
  90.7 0.1 collective-permute-start.13
  90.8 0.0 collective-permute-done.15.refs_4_
  90.8 5.6 %shard_map.20 = (f32[1,512]{1,0:T(1,128)S(1)}, f32[1,512]{1,0:T(1,128)S(1)}, f32[1,512]{1,0:T(1,128)S(1)}, f32[1,512]{1,0:T(1,128)S(1)}, f32[1,512]{1,0:T(1,128)...) custom-call(s32[1]{0:T(128)} %bitcast.flag, bf16[512,1024]{1,0:T(8,128)(2,1)S(1)} %collective-permute-done.14.refs_0_.refs_1_, ...), custom_call_target="tpu_custom_call" | custom-call | flops 1 | bytes 1 | tf_op jit(solution)/shard_map/pallas_call | solution.py:219
  96.4 6.4 %collective-permute-start.16 = (f32[1024]{0:T(1024)S(1)}, f32[1024]{0:T(1024)S(1)}, u32[]{:S(2)}, u32[]{:S(2)}) collective-permute-start(f32[1024]{0:T(1024)S(1)} %pad_maximum_fusion.3), channel_id=1, source_target_pairs={{6,0},{3,1},{38,32},{59,33},{0,2},{5,3},{32,34},{61,35},{10,4},{7,... | collective-permute-start | bytes 12296 | tf_op jit(solution)/shard_map/ppermute | solution.py:102
  102.8 0.0 collective-permute-done.17.refs_2_
  102.9 4.3 %collective-permute-start.18 = (f32[1024]{0:T(1024)S(1)}, f32[1024]{0:T(1024)S(1)}, u32[]{:S(2)}, u32[]{:S(2)}) collective-permute-start(f32[1024]{0:T(1024)S(1)} %pad_maximum_fusion.4), channel_id=1, source_target_pairs={{32,0},{39,1},{2,32},{25,33},{34,2},{33,3},{4,34},{3,35},{36,4},{3... | collective-permute-start | bytes 12296 | tf_op jit(solution)/shard_map/ppermute | solution.py:102
  107.3 0.1 collective-permute-start.19
  107.4 0.0 collective-permute-done.13
  107.4 1.2 %collective-permute-done.18 = f32[1024]{0:T(1024)S(1)} collective-permute-done((f32[1024]{0:T(1024)S(1)}, f32[1024]{0:T(1024)S(1)}, u32[]{:S(2)}, u32[]{:S(2)}) %collective-permute-start.18) | collective-permute-done | bytes 4128 | tf_op jit(solution)/shard_map/ppermute | solution.py:102
  108.6 6.6 %collective-permute-done.19 = f32[1024]{0:T(1024)S(1)} collective-permute-done((f32[1024]{0:T(1024)S(1)}, f32[1024]{0:T(1024)S(1)}, u32[]{:S(2)}, u32[]{:S(2)}) %collective-permute-start.19) | collective-permute-done | bytes 4128 | tf_op jit(solution)/shard_map/ppermute | solution.py:102
  115.2 0.6 fusion.7
  (18 shorter events, 0.1 us)
Async XLA Ops:
  0.0 1.9 %copy-start = (bf16[1024,1024]{1,0:T(8,128)(2,1)S(1)}, bf16[1024,1024]{1,0:T(8,128)(2,1)}, u32[]{:S(2)}) copy-start(bf16[1024,1024]{1,0:T(8,128)(2,1)} %refs_0_.1) | copy-start | bytes 6291460
  3.0 30.9 %collective-permute-start.1 = (bf16[1024,1024]{1,0:T(8,128)(2,1)S(1)}, bf16[1024,1024]{1,0:T(8,128)(2,1)}, u32[]{:S(2)}, u32[]{:S(2)}) collective-permute-start(bf16[1024,1024]{1,0:T(8,128)(2,1)S(1)} %copy-done), channel_id=1, source_target_pairs={{1,217},{32,96},{33,57},{3,195},{34,98},{5,197},{36,100},{6,14},{7... | collective-permute-start | bytes 6291464 | tf_op jit(solution)/shard_map/ppermute | solution.py:102
  4.9 15.4 %collective-permute-start.2 = (bf16[512,1024]{1,0:T(8,128)(2,1)S(1)}, bf16[512,1024]{1,0:T(8,128)(2,1)}, u32[]{:S(2)}, u32[]{:S(2)}) collective-permute-start(bf16[512,1024]{1,0:T(8,128)(2,1)S(1)} %slice.16), channel_id=1, source_target_pairs={{0,38},{1,33},{32,0},{33,3},{2,32},{3,35},{34,2},{35,5},{4,34},{5,... | collective-permute-start | bytes 3145736 | tf_op jit(solution)/shard_map/ppermute | solution.py:102
  6.5 25.0 %collective-permute-start.5 = (bf16[512,1024]{1,0:T(8,128)(2,1)}, bf16[512,1024]{1,0:T(8,128)(2,1)}, u32[]{:S(2)}, u32[]{:S(2)}) collective-permute-start(bf16[512,1024]{1,0:T(8,128)(2,1)} %slice.17), channel_id=1, source_target_pairs={{0,38},{1,33},{32,0},{33,3},{2,32},{3,35},{34,2},{35,5},{4,34},{5,... | collective-permute-start | bytes 3145736 | tf_op jit(solution)/shard_map/ppermute | solution.py:102
  6.6 63.7 %collective-permute-start = (bf16[1024,1024]{1,0:T(8,128)(2,1)S(1)}, bf16[1024,1024]{1,0:T(8,128)(2,1)}, u32[]{:S(2)}, u32[]{:S(2)}) collective-permute-start(bf16[1024,1024]{1,0:T(8,128)(2,1)S(1)} %copy-done), channel_id=1, source_target_pairs={{0,1},{1,0},{32,57},{33,32},{2,3},{3,10},{34,59},{35,34},{4,5},{5,... | collective-permute-start | bytes 6291464 | tf_op jit(solution)/shard_map/ppermute | solution.py:102
  20.3 24.9 %collective-permute-start.3 = (bf16[512,1024]{1,0:T(8,128)(2,1)}, bf16[512,1024]{1,0:T(8,128)(2,1)S(1)}, u32[]{:S(2)}, u32[]{:S(2)}) collective-permute-start(bf16[512,1024]{1,0:T(8,128)(2,1)} %collective-permute-done.2.refs_1_), channel_id=1, source_target_pairs={{0,38},{1,33},{32,0},{33,3},{2,32},{3,59},{34,10},{35,5},{4,34},{5... | collective-permute-start | bytes 3145736 | tf_op jit(solution)/shard_map/ppermute | solution.py:102
  31.6 31.5 %collective-permute-start.6 = (bf16[512,1024]{1,0:T(8,128)(2,1)}, bf16[512,1024]{1,0:T(8,128)(2,1)S(1)}, u32[]{:S(2)}, u32[]{:S(2)}) collective-permute-start(bf16[512,1024]{1,0:T(8,128)(2,1)} %collective-permute-done.5.refs_2_), channel_id=1, source_target_pairs={{0,38},{1,33},{32,0},{33,3},{2,32},{3,59},{34,10},{35,5},{4,34},{5... | collective-permute-start | bytes 3145736 | tf_op jit(solution)/shard_map/ppermute | solution.py:102
  45.3 22.0 %collective-permute-start.4 = (bf16[512,1024]{1,0:T(8,128)(2,1)S(1)}, bf16[512,1024]{1,0:T(8,128)(2,1)S(1)}, u32[]{:S(2)}, u32[]{:S(2)}) collective-permute-start(bf16[512,1024]{1,0:T(8,128)(2,1)S(1)} %get-tuple-element.46), channel_id=1, source_target_pairs={{0,32},{1,39},{32,2},{33,1},{2,34},{3,33},{34,4},{35,3},{4,36},{5,... | collective-permute-start | bytes 3145736 | tf_op jit(solution)/shard_map/ppermute | solution.py:102
  45.3 23.3 %collective-permute-start.11 = (bf16[512,1024]{1,0:T(8,128)(2,1)S(1)}, bf16[512,1024]{1,0:T(8,128)(2,1)S(1)}, u32[]{:S(2)}, u32[]{:S(2)}) collective-permute-start(bf16[512,1024]{1,0:T(8,128)(2,1)S(1)} %collective-permute-done.3.refs_2_.refs_1_), channel_id=1, source_target_pairs={{0,216},{33,105},{2,218},{35,107},{4,220},{37,109},{6,222},{39,111... | collective-permute-start | bytes 3145736 | tf_op jit(solution)/shard_map/ppermute | solution.py:102
  50.8 26.0 %collective-permute-start.7 = (bf16[512,1024]{1,0:T(8,128)(2,1)S(1)}, bf16[512,1024]{1,0:T(8,128)(2,1)S(1)}, u32[]{:S(2)}, u32[]{:S(2)}) collective-permute-start(bf16[512,1024]{1,0:T(8,128)(2,1)S(1)} %collective-permute-done.3.refs_2_.refs_1_), channel_id=1, source_target_pairs={{1,8},{32,57},{3,10},{34,59},{5,12},{36,61},{7,14},{38,63},{9,16},... | collective-permute-start | bytes 3145736 | tf_op jit(solution)/shard_map/ppermute | solution.py:102
  63.0 21.0 %collective-permute-start.10 = (bf16[512,1024]{1,0:T(8,128)(2,1)S(1)}, bf16[512,1024]{1,0:T(8,128)(2,1)S(1)}, u32[]{:S(2)}, u32[]{:S(2)}) collective-permute-start(bf16[512,1024]{1,0:T(8,128)(2,1)S(1)} %collective-permute-done.6.refs_3_.refs_2_), channel_id=1, source_target_pairs={{1,8},{32,57},{3,10},{34,59},{5,12},{36,61},{7,14},{38,63},{9,16},... | collective-permute-start | bytes 3145736 | tf_op jit(solution)/shard_map/ppermute | solution.py:102
  67.2 16.9 %collective-permute-start.12 = (bf16[512,1024]{1,0:T(8,128)(2,1)S(1)}, bf16[512,1024]{1,0:T(8,128)(2,1)S(1)}, u32[]{:S(2)}, u32[]{:S(2)}) collective-permute-start(bf16[512,1024]{1,0:T(8,128)(2,1)S(1)} %collective-permute-done.4.refs_0_.refs_5_), channel_id=1, source_target_pairs={{0,1},{33,32},{2,3},{35,34},{4,5},{37,36},{6,7},{39,38},{8,9},{41,... | collective-permute-start | bytes 3145736 | tf_op jit(solution)/shard_map/ppermute | solution.py:102
  68.6 20.6 %collective-permute-start.14 = (bf16[512,1024]{1,0:T(8,128)(2,1)S(1)}, bf16[512,1024]{1,0:T(8,128)(2,1)S(1)}, u32[]{:S(2)}, u32[]{:S(2)}) collective-permute-start(bf16[512,1024]{1,0:T(8,128)(2,1)S(1)} %get-tuple-element.63), channel_id=1, source_target_pairs={{0,32},{1,39},{32,2},{33,1},{2,34},{3,33},{34,4},{35,3},{4,36},{5,... | collective-permute-start | bytes 3145736 | tf_op jit(solution)/shard_map/ppermute | solution.py:102
  70.3 20.5 %collective-permute-start.15 = (bf16[512,1024]{1,0:T(8,128)(2,1)S(1)}, bf16[512,1024]{1,0:T(8,128)(2,1)S(1)}, u32[]{:S(2)}, u32[]{:S(2)}) collective-permute-start(bf16[512,1024]{1,0:T(8,128)(2,1)S(1)} %collective-permute-done.6.refs_3_.refs_2_), channel_id=1, source_target_pairs={{0,216},{33,105},{2,218},{35,107},{4,220},{37,109},{6,222},{39,111... | collective-permute-start | bytes 3145736 | tf_op jit(solution)/shard_map/ppermute | solution.py:102
  76.8 12.4 %collective-permute-start.8 = (f32[1024]{0:T(1024)S(1)}, f32[1024]{0:T(1024)S(1)}, u32[]{:S(2)}, u32[]{:S(2)}) collective-permute-start(f32[1024]{0:T(1024)S(1)} %pad_maximum_fusion), channel_id=1, source_target_pairs={{217,1},{96,32},{195,3},{98,34},{197,5},{100,36},{199,7},{110,38},... | collective-permute-start | bytes 12296 | tf_op jit(solution)/shard_map/ppermute | solution.py:102
  84.0 5.2 %collective-permute-start.9 = (f32[1024]{0:T(1024)S(1)}, f32[1024]{0:T(1024)S(1)}, u32[]{:S(2)}, u32[]{:S(2)}) collective-permute-start(f32[1024]{0:T(1024)S(1)} %pad_maximum_fusion.1), channel_id=1, source_target_pairs={{1,0},{0,1},{57,32},{32,33},{3,2},{10,3},{59,34},{34,35},{5,4},{12... | collective-permute-start | bytes 12296 | tf_op jit(solution)/shard_map/ppermute | solution.py:102
  89.3 13.6 %collective-permute-start.17 = (bf16[512,1024]{1,0:T(8,128)(2,1)S(1)}, bf16[512,1024]{1,0:T(8,128)(2,1)S(1)}, u32[]{:S(2)}, u32[]{:S(2)}) collective-permute-start(bf16[512,1024]{1,0:T(8,128)(2,1)S(1)} %collective-permute-done.14.refs_0_.refs_1_), channel_id=1, source_target_pairs={{0,1},{33,32},{2,3},{35,34},{4,5},{37,36},{6,7},{39,38},{8,9},{41,... | collective-permute-start | bytes 3145736 | tf_op jit(solution)/shard_map/ppermute | solution.py:102
  90.7 16.7 %collective-permute-start.13 = (f32[1024]{0:T(1024)S(1)}, f32[1024]{0:T(1024)S(1)}, u32[]{:S(2)}, u32[]{:S(2)}) collective-permute-start(f32[1024]{0:T(1024)S(1)} %pad_maximum_fusion.2), channel_id=1, source_target_pairs={{38,0},{3,33},{32,2},{5,35},{34,4},{7,37},{36,6},{1,39},{46,8},{11... | collective-permute-start | bytes 12296 | tf_op jit(solution)/shard_map/ppermute | solution.py:102
  96.4 10.9 %collective-permute-start.16 = (f32[1024]{0:T(1024)S(1)}, f32[1024]{0:T(1024)S(1)}, u32[]{:S(2)}, u32[]{:S(2)}) collective-permute-start(f32[1024]{0:T(1024)S(1)} %pad_maximum_fusion.3), channel_id=1, source_target_pairs={{6,0},{3,1},{38,32},{59,33},{0,2},{5,3},{32,34},{61,35},{10,4},{7,... | collective-permute-start | bytes 12296 | tf_op jit(solution)/shard_map/ppermute | solution.py:102
  102.9 5.6 %collective-permute-start.18 = (f32[1024]{0:T(1024)S(1)}, f32[1024]{0:T(1024)S(1)}, u32[]{:S(2)}, u32[]{:S(2)}) collective-permute-start(f32[1024]{0:T(1024)S(1)} %pad_maximum_fusion.4), channel_id=1, source_target_pairs={{32,0},{39,1},{2,32},{25,33},{34,2},{33,3},{4,34},{3,35},{36,4},{3... | collective-permute-start | bytes 12296 | tf_op jit(solution)/shard_map/ppermute | solution.py:102
  107.3 7.9 %collective-permute-start.19 = (f32[1024]{0:T(1024)S(1)}, f32[1024]{0:T(1024)S(1)}, u32[]{:S(2)}, u32[]{:S(2)}) collective-permute-start(f32[1024]{0:T(1024)S(1)} %pad_maximum_fusion.5), channel_id=1, source_target_pairs={{38,1},{3,32},{32,3},{5,34},{34,5},{7,36},{36,7},{1,38},{46,9},{11... | collective-permute-start | bytes 12296 | tf_op jit(solution)/shard_map/ppermute | solution.py:102
